TPU v7x, 128 devices: a whole 4x4x4 slice. The times are simulated.
128 devices in a mesh: lat: 8 (over z_hi, x), lon: 16 (over z_lo, y, core).
Axes of the slice: x: 4, y: 4, z: 4 (z_hi: 2, z_lo: 2; z = z_hi * 2 + z_lo), core: 2. Of those that a mesh axis runs over, the one named last changes fastest.
Arguments:
- thickness: float32 [32, 2880, 1024], P(None, 'lon', 'lat'), may hold values from 0.5 to 1.5
- tracer_mass: float32 [32, 2880, 1024], P(None, 'lon', 'lat'), may hold values from -6 to 6
- zonal_courant: float32 [32, 2880, 1024], P(None, 'lon', 'lat'), may hold values from -0.45 to 0.45
- merid_courant: float32 [32, 2880, 1024], P(None, 'lon', 'lat'), may hold values from -0.45 to 0.45
- cutoffs: int32 [512], replicated, may hold values from 32 to 256, as said below
Outputs:
- thickness_out: float32 [32, 2880, 1024], P(None, 'lon', 'lat')
- tracer_out: float32 [32, 2880, 1024], P(None, 'lon', 'lat')
Inputs may be any that keep to these rules, and one draw needn't show every extreme that they name: Both ends 256 // 8 and 256 occur among the cutoffs.
All inputs are finite; a program needn't handle non-finite values.
Results may differ from a plain program's by a relative error of at most 0.0001.
Values sent between devices are 32-bit elements; how exact they have to be, the bound alone decides.
A program may use at most 256 MiB of HBM per device.

v0:
```python
import math

import jax
import jax.numpy as jnp
from jax import lax
from jax.sharding import PartitionSpec as P

KW = 256
SUBSTEPS = 2


def extended(value, sides, width):
    for axis, dim in sides:
        devices, length = (lax.axis_size(axis), value.shape[dim])
        up = [(i, (i + 1) % devices) for i in range(devices)]
        down = [(j, i) for i, j in up]
        last = lax.slice_in_dim(value, length - width, length, axis=dim)
        first = lax.slice_in_dim(value, 0, width, axis=dim)
        before = lax.ppermute(last, axis, up)
        after = lax.ppermute(first, axis, down)
        value = jnp.concatenate([before, value, after], axis=dim)
    return value


def passed_along(block, axis, distance):
    devices = range(lax.axis_size(axis))
    route = [((i - distance) % len(devices), i) for i in devices]
    return lax.ppermute(block, axis, route)


def upwind(
    centre,
    east_field,
    west_field,
    north_field,
    south_field,
    zonal,
    east_zonal,
    west_zonal,
    merid,
    north_merid,
    south_merid,
):
    face_east = 0.5 * (zonal + east_zonal)
    face_west = 0.5 * (west_zonal + zonal)
    face_north = 0.5 * (merid + north_merid)
    face_south = 0.5 * (south_merid + merid)
    flux_east = jnp.maximum(face_east, 0.0) * centre + jnp.minimum(face_east, 0.0) * east_field
    flux_west = jnp.maximum(face_west, 0.0) * west_field + jnp.minimum(face_west, 0.0) * centre
    flux_north = jnp.maximum(face_north, 0.0) * centre + jnp.minimum(face_north, 0.0) * north_field
    flux_south = jnp.maximum(face_south, 0.0) * south_field + jnp.minimum(face_south, 0.0) * centre
    return centre - (flux_east - flux_west) - (flux_north - flux_south)


def fix_rims(padded, across, factor, at_south, at_north):
    south_rim = jnp.where(at_south, factor * across[0], padded[..., 1:-1, 0])
    north_rim = jnp.where(at_north, factor * across[1], padded[..., 1:-1, -1])
    padded = padded.at[..., 1:-1, 0].set(south_rim)
    return padded.at[..., 1:-1, -1].set(north_rim)


def row_cutoffs(cutoffs, source_band, lat_rows, total_lat):
    latitude = source_band * lat_rows + jnp.arange(lat_rows, dtype=jnp.int32)
    polar_index = jnp.where(latitude < total_lat // 4, latitude, latitude - total_lat // 2)
    slots = jnp.arange(cutoffs.shape[0], dtype=jnp.int32)
    return jnp.sum(jnp.where(polar_index[:, None] == slots[None, :], cutoffs[None, :], 0), axis=1)


def apply_filter(segment_rows, row_cut, dft_table, wave_weight):
    spectrum = jnp.einsum(
        "pk,ilpr->ilkr",
        dft_table,
        segment_rows,
        precision=lax.Precision.HIGHEST,
        preferred_element_type=jnp.float32,
    )
    wave_index = jnp.arange(wave_weight.shape[0], dtype=jnp.int32)
    keep_weight = jnp.where(wave_index[:, None] < row_cut[None, :], wave_weight[:, None], 0.0)
    keep_weight = jnp.concatenate([keep_weight, keep_weight], axis=0)
    spectrum = spectrum * keep_weight
    return jnp.einsum(
        "pk,ilkr->ilpr",
        dft_table,
        spectrum,
        precision=lax.Precision.HIGHEST,
        preferred_element_type=jnp.float32,
    )


def on_device(thickness, tracer_mass, zonal_courant, merid_courant, cutoffs):
    lat_size = lax.axis_size("lat")
    lon_size = lax.axis_size("lon")
    lat_band = lax.axis_index("lat")
    levels, columns, lat_rows = thickness.shape
    points = columns * lon_size
    total_lat = lat_rows * lat_size
    quarter = lat_size // 4
    is_polar = (lat_band < quarter) | (lat_band >= lat_size - quarter)
    at_south = lat_band == 0
    at_north = lat_band == lat_size - 1
    longitude = jnp.arange(points, dtype=jnp.int32)
    wave_index = jnp.arange(KW, dtype=jnp.int32)
    phase = (longitude[:, None] * wave_index[None, :] % points).astype(jnp.float32) * (
        2.0 * math.pi / points
    )
    dft_table = jnp.concatenate([jnp.cos(phase), jnp.sin(phase)], axis=1)
    wave_weight = (jnp.where(wave_index == 0, 1.0, 2.0) / points).astype(jnp.float32)
    own_cut = row_cutoffs(cutoffs, lat_band, lat_rows, total_lat)
    winds = jnp.stack([zonal_courant, merid_courant])
    fields = jnp.stack([thickness, tracer_mass])
    wind_pad = extended(winds, (("lat", 3), ("lon", 2)), 1)
    wind_edges = jnp.stack([merid_courant[..., 0], merid_courant[..., -1]])
    wind_across = passed_along(wind_edges, "lon", lon_size // 2)
    merid_pad = fix_rims(wind_pad[1], wind_across, -1.0, at_south, at_north)
    zonal_pad = wind_pad[0]
    zonal = zonal_pad[:, 1:-1, 1:-1]
    east_zonal = zonal_pad[:, 2:, 1:-1]
    west_zonal = zonal_pad[:, :-2, 1:-1]
    merid = merid_pad[:, 1:-1, 1:-1]
    north_merid = merid_pad[:, 1:-1, 2:]
    south_merid = merid_pad[:, 1:-1, :-2]
    for substep in range(SUBSTEPS):
        padded = extended(fields, (("lat", 3), ("lon", 2)), 1)
        edge_rows = jnp.stack([fields[..., 0], fields[..., -1]])
        across = passed_along(edge_rows, "lon", lon_size // 2)
        padded = fix_rims(padded, across, 1.0, at_south, at_north)
        advected = upwind(
            padded[:, :, 1:-1, 1:-1],
            padded[:, :, 2:, 1:-1],
            padded[:, :, :-2, 1:-1],
            padded[:, :, 1:-1, 2:],
            padded[:, :, 1:-1, :-2],
            zonal,
            east_zonal,
            west_zonal,
            merid,
            north_merid,
            south_merid,
        )
        spread = lax.cond(
            is_polar,
            lambda inner_rows: apply_filter(inner_rows, own_cut, dft_table, wave_weight),
            lambda inner_rows: inner_rows,
            lax.all_to_all(advected, "lon", split_axis=1, concat_axis=2, tiled=True),
        )
        filtered = lax.all_to_all(spread, "lon", split_axis=2, concat_axis=1, tiled=True)
        fields = filtered
    return (fields[0], fields[1])


def solution(mesh):
    placed = (
        P(None, "lon", "lat"),
        P(None, "lon", "lat"),
        P(None, "lon", "lat"),
        P(None, "lon", "lat"),
        P(),
    )
    return jax.shard_map(
        on_device,
        mesh=mesh,
        in_specs=placed,
        out_specs=(P(None, "lon", "lat"), P(None, "lon", "lat")),
        check_vma=False,
    )
```

profile of v0, /device:TPU:1, one launch (start us, length us, event | category | flops | bytes accessed | tf_op | source)
XLA Modules:
  0.0 738.7 jit_solution(11195237467170653007)
XLA Ops:
  0.6 5.4 copy.139
  6.8 2.5 collective-permute-start.9
  9.3 3.8 copy.132
  13.1 5.2 copy.133
  20.5 4.4 collective-permute-start.1
  24.9 3.7 copy.138
  29.5 5.1 collective-permute-start.6
  36.2 4.0 pad_maximum_fusion.4
  40.2 4.9 fusion.63
  45.1 4.8 copy.140
  50.0 4.8 copy.141
  54.8 2.4 collective-permute-start.8
  58.7 4.0 pad_maximum_fusion.2
  62.8 4.9 fusion.64
  67.7 4.8 copy.134
  72.5 4.9 copy.135
  79.2 5.9 copy.142
  85.0 5.8 copy.143
  90.8 9.2 %pad_maximum_fusion.5 = f32[2,32,182,130]{2,1,3,0:T(8,128)S(1)} fusion(f32[2,32,1,130]{2,1,3,0:T(8,128)} %copy.143, f32[2,32,180,1]{2,1,3,0:T(8,128)S(1)} %collective-permute-done.6, f32[1,32,180,128]{2,1,3,0:T(8,128)} %bitcast.107, f32[1,32,180,128]{2,1,3,0:T(8,128)} %bitcast.116, f32[2,32,180,1]{2,1,3,0:T(8,128)S(1)} %collective-permute-done.5, ...), kind=kLoop, calls=%fused_computation.23 | loop fusion | flops 7571200 | bytes 12113920 | tf_op jit(solution)/shard_map/concatenate | solution.py:21
  100.0 3.3 slice_bitcast_fusion.1
  103.3 2.0 copy-done
  108.4 22.4 %broadcast_maximum_fusion.1 = (f32[32,180,128]{1,0,2:T(8,128)}, f32[32,180,128]{1,0,2:T(8,128)}, f32[32,180,128]{1,0,2:T(8,128)}, f32[32,180,128]{1,0,2:T(8,128)...) fusion(f32[32,182,130]{1,0,2:T(8,128)} %scatter.25, ...), kind=kLoop, calls=%fused_computation.74 | loop fusion | flops 11796480 | bytes 41287680 | tf_op jit(solution)/shard_map/max | solution.py:50
  130.8 5.9 copy.136
  136.7 5.9 copy.137
  142.6 11.7 %pad_maximum_fusion.3 = f32[2,32,182,130]{2,1,0,3:T(8,128)} fusion(f32[2,32,1,130]{2,1,0,3:T(8,128)} %copy.137, f32[2,32,180,1]{2,1,0,3:T(8,128)S(1)} %collective-permute-done.1, f32[1,32,180,128]{2,1,0,3:T(8,128)} %bitcast.113, f32[1,32,180,128]{2,1,0,3:T(8,128)} %bitcast.110, f32[2,32,180,1]{2,1,0,3:T(8,128)S(1)} %collective-permute-done, ...), kind=kLoop, calls=%fused_computation.21 | loop fusion | flops 7571200 | bytes 12113920 | tf_op jit(solution)/shard_map/concatenate | solution.py:21
  154.3 1.7 scatter.20
  157.6 33.9 %fusion.38 = f32[2,32,180,128]{2,1,0,3:T(8,128)} fusion(f32[2,32,182,130]{2,1,0,3:T(8,128)} %scatter.21, f32[32,180,128]{1,0,2:T(8,128)} %get-tuple-element.139, f32[32,180,128]{1,0,2:T(8,128)} %get-tuple-element.141, f32[32,180,128]{1,0,2:T(8,128)} %get-tuple-element.140, f32[32,180,128]{1,0,2:T(8,128)} %get-tuple-element.138, ...), kind=kLoop, calls=%fused_computation.41 | loop fusion | flops 23592960 | bytes 58982400 | tf_op jit(solution)/shard_map/sub | solution.py:52
  191.5 9.3 %copy.146 = f32[2,32,180,128]{3,0,2,1:T(2,128)} copy(f32[2,32,180,128]{2,1,0,3:T(8,128)} %fusion.38) | data formatting | bytes 11796480 | tf_op jit(solution)/shard_map/sub | solution.py:52
  200.9 8.2 %all-to-all-start = ((f32[2,32,180,128]{3,0,2,1:T(2,128)}), f32[2,32,180,128]{3,0,2,1:T(2,128)}, u32[]{:S(2)}, u32[]{:S(2)}) async-start(f32[2,32,180,128]{3,0,2,1:T(2,128)} %copy.146), calls=%async_computation | async-start | bytes 11796480 | tf_op jit(solution)/shard_map/all_to_all | solution.py:144
  209.2 12.4 %fusion.52 = (f32[2880,256]{1,0:T(8,128)S(1)}, f32[2880,256]{1,0:T(8,128)S(1)}) fusion(), kind=kLoop, calls=%fused_computation.68 | loop fusion | flops 6635520 | bytes 5898240 | tf_op jit(solution)/shard_map/sin | solution.py:106
  221.6 3.5 pad_maximum_fusion.8
  225.1 62.7 %all-to-all-done = f32[2,32,180,128]{3,0,2,1:T(2,128)} async-done(((f32[2,32,180,128]{3,0,2,1:T(2,128)}), f32[2,32,180,128]{3,0,2,1:T(2,128)}, u32[]{:S(2)}, u32[]{:S(2)}) %all-to-all-start) | async-done | bytes 5898272 | tf_op jit(solution)/shard_map/all_to_all | solution.py:144
  287.7 3.1 copy.147
  290.8 3.0 copy.148
  293.8 6.9 all_to_all.59
  300.6 26.4 %conditional.2 = (f32[2,2,2880,128]{3,2,1,0:T(8,128)}) conditional(s32[]{:T(128)} %convert_element_type.9, f32[2,2,2880,128]{3,2,1,0:T(8,128)} %all_to_all.59, (f32[2,2,2880,128]{3,2,1,0:T(8,128)}, f32[2880,512]{1,0:T(8,128)}, s32[128]{0:T(128)S(1)}, f32[256]{0:T(256)S(1)}) %tuple.44), branch_computations={%region_1.2_spmd, %region_2.3_spmd} | conditional | flops 18119786496 | bytes 44172856 | solution.py:140
  300.8 14.5 %fusion.10 = f32[2,2,512,128]{2,3,1,0:T(8,128)S(1)} fusion(f32[2,2,2880,128]{3,2,1,0:T(8,128)} %get-tuple-element.96, f32[2880,512]{1,0:T(8,128)} %get-tuple-element.97, f32[512,128]{0,1:T(8,128)S(1)} %pad_maximum_fusion), kind=kOutput, calls=%fused_computation.6 | convolution fusion | flops 9059958784 | bytes 13107200 | tf_op jit(solution)/shard_map/cond/branch_1_fun/pk,ilpr->ilkr/dot_general | solution.py:70
  315.3 11.4 %fusion.4 = f32[2,2,2880,128]{3,2,1,0:T(8,128)} fusion(f32[2,2,512,128]{2,3,1,0:T(8,128)S(1)} %fusion.10, f32[2880,512]{1,0:T(8,128)S(1)} %bitcast.102), kind=kOutput, calls=%fused_computation.4 | convolution fusion | flops 9059696640 | bytes 12845056 | tf_op jit(solution)/shard_map/cond/branch_1_fun/pk,ilkr->ilpr/dot_general | solution.py:81
  327.1 17.2 %copy.149 = f32[2,2,2880,128]{3,1,0,2:T(2,128)S(1)} copy(f32[2,2,2880,128]{3,2,1,0:T(8,128)} %get-tuple-element.154) | data formatting | bytes 11796480 | tf_op jit(solution)/shard_map/cond | solution.py:140
  344.3 73.1 %all_to_all.75 = f32[2,2,2880,128]{3,1,0,2:T(2,128)S(1)} all-to-all(f32[2,2,2880,128]{3,1,0,2:T(2,128)S(1)} %copy.149), channel_id=1, replica_groups=mesh['lat'=8,'lon'=16] {'lon'}, dimensions={2} | all-to-all | bytes 11796480 | tf_op jit(solution)/shard_map/all_to_all | solution.py:146
  417.4 3.0 copy.173
  420.5 9.4 %copy.152 = f32[2,32,180,128]{2,1,0,3:T(8,128)} copy(f32[2,32,180,128]{3,2,1,0:T(8,128)} %bitcast.117) | data formatting | bytes 11796480 | tf_op jit(solution)/shard_map/all_to_all | solution.py:146
  430.7 3.6 collective-permute-start.11
  435.6 5.4 collective-permute-done.10
  441.0 3.9 pad_maximum_fusion.6
  445.0 4.9 fusion.62
  449.8 4.8 copy.155
  454.7 4.9 copy.156
  459.6 2.0 collective-permute-start.13
  463.5 5.8 copy.157
  469.4 5.8 copy.158
  475.2 10.7 %pad_maximum_fusion.7 = f32[2,32,182,130]{2,1,0,3:T(8,128)} fusion(f32[2,32,1,130]{2,1,0,3:T(8,128)} %copy.158, f32[2,32,180,1]{2,1,0,3:T(8,128)S(1)} %collective-permute-done.11, f32[2,32,180,128]{2,1,0,3:T(8,128)} %copy.152, f32[2,32,180,1]{2,1,0,3:T(8,128)S(1)} %collective-permute-done.10, f32[2,32,1,130]{2,1,0,3:T(8,128)} %copy.157), kind=kLoop, calls=%fused_computation.25 | loop fusion | flops 6056960 | bytes 12113920 | tf_op jit(solution)/shard_map/concatenate | solution.py:21
  489.2 33.9 %fusion.30 = f32[2,32,180,128]{2,1,0,3:T(8,128)} fusion(f32[2,32,182,130]{2,1,0,3:T(8,128)} %scatter.29, f32[32,180,128]{1,0,2:T(8,128)} %get-tuple-element.139, f32[32,180,128]{1,0,2:T(8,128)} %get-tuple-element.141, f32[32,180,128]{1,0,2:T(8,128)} %get-tuple-element.140, f32[32,180,128]{1,0,2:T(8,128)} %get-tuple-element.138, ...), kind=kLoop, calls=%fused_computation.29 | loop fusion | flops 23592960 | bytes 58982400 | tf_op jit(solution)/shard_map/sub | solution.py:52
  523.1 9.3 %copy.159 = f32[2,32,180,128]{3,0,2,1:T(2,128)} copy(f32[2,32,180,128]{2,1,0,3:T(8,128)} %fusion.30) | data formatting | bytes 11796480 | tf_op jit(solution)/shard_map/sub | solution.py:52
  532.4 75.6 %all_to_all.76 = f32[2,32,180,128]{3,0,2,1:T(2,128)S(1)} all-to-all(f32[2,32,180,128]{3,0,2,1:T(2,128)} %copy.159), channel_id=1, replica_groups=mesh['lat'=8,'lon'=16] {'lon'}, dimensions={1} | all-to-all | bytes 11796480 | tf_op jit(solution)/shard_map/all_to_all | solution.py:144
  608.4 3.0 copy.161
  611.4 6.9 all_to_all.67
  618.2 26.5 %conditional.3 = (f32[2,2,2880,128]{3,2,1,0:T(8,128)}) conditional(s32[]{:T(128)} %convert_element_type.9, f32[2,2,2880,128]{3,2,1,0:T(8,128)} %all_to_all.67, (f32[2,2,2880,128]{3,2,1,0:T(8,128)}, f32[2880,512]{1,0:T(8,128)}, s32[128]{0:T(128)S(1)}, f32[256]{0:T(256)S(1)}) %tuple.45), branch_computations={%region_3.4_spmd, %region_4.5_spmd} | conditional | flops 18119786496 | bytes 44172856 | solution.py:140
  618.6 14.5 %fusion.24 = f32[2,2,512,128]{2,3,1,0:T(8,128)S(1)} fusion(f32[2,2,2880,128]{3,2,1,0:T(8,128)} %get-tuple-element.100, f32[2880,512]{1,0:T(8,128)} %get-tuple-element.101, f32[512,128]{0,1:T(8,128)S(1)} %pad_maximum_fusion.1), kind=kOutput, calls=%fused_computation.16 | convolution fusion | flops 9059958784 | bytes 13107200 | tf_op jit(solution)/shard_map/cond/branch_1_fun/pk,ilpr->ilkr/dot_general | solution.py:70
  633.1 11.4 %fusion.18 = f32[2,2,2880,128]{3,2,1,0:T(8,128)} fusion(f32[2,2,512,128]{2,3,1,0:T(8,128)S(1)} %fusion.24, f32[2880,512]{1,0:T(8,128)S(1)} %bitcast.104), kind=kOutput, calls=%fused_computation.14 | convolution fusion | flops 9059696640 | bytes 12845056 | tf_op jit(solution)/shard_map/cond/branch_1_fun/pk,ilkr->ilpr/dot_general | solution.py:81
  644.7 17.2 %copy.162 = f32[2,2,2880,128]{3,1,0,2:T(2,128)S(1)} copy(f32[2,2,2880,128]{3,2,1,0:T(8,128)} %get-tuple-element.155) | data formatting | bytes 11796480 | tf_op jit(solution)/shard_map/cond | solution.py:140
  661.9 70.8 %all_to_all.77 = f32[2,2,2880,128]{3,1,0,2:T(2,128)S(1)} all-to-all(f32[2,2,2880,128]{3,1,0,2:T(2,128)S(1)} %copy.162), channel_id=1, replica_groups=mesh['lat'=8,'lon'=16] {'lon'}, dimensions={2} | all-to-all | bytes 11796480 | tf_op jit(solution)/shard_map/all_to_all | solution.py:146
  733.8 2.1 copy.167
  736.2 2.1 copy.166
  (67 shorter events, 23.1 us)
Async XLA Ops:
  0.6 8.7 %copy-start.1 = (f32[32,180,128]{2,0,1:T(8,128)S(1)}, f32[32,180,128]{2,0,1:T(8,128)}, u32[]{:S(2)}) copy-start(f32[32,180,128]{2,0,1:T(8,128)} %param.21) | copy-start | bytes 8847364
  6.8 96.5 %collective-permute-start.9 = (f32[2,32,180]{2,1,0:T(8,128)S(1)}, f32[2,32,180]{2,1,0:T(8,128)S(1)}, u32[]{:S(2)}, u32[]{:S(2)}) collective-permute-start(f32[2,32,180]{2,1,0:T(8,128)S(1)} %pad_maximum_fusion.15), channel_id=1, source_target_pairs={{8,0},{9,1},{10,2},{11,3},{12,4},{13,5},{14,6},{15,7},{0,8},{1,9},... | collective-permute-start | bytes 138248 | tf_op jit(solution)/shard_map/ppermute | solution.py:28
  18.3 6.6 copy-start.2
  19.2 38.0 %collective-permute-start = (f32[2,32,180,1]{2,1,0,3:T(8,128)S(1)}, f32[2,32,180,1]{2,1,0,3:T(8,128)S(1)}, u32[]{:S(2)}, u32[]{:S(2)}) collective-permute-start(f32[2,32,180,1]{2,1,0,3:T(8,128)S(1)} %get-tuple-element.128), channel_id=1, source_target_pairs={{0,16},{16,32},{32,48},{48,64},{64,80},{80,96},{96,112},{112,0},{1... | collective-permute-start | bytes 138248 | tf_op jit(solution)/shard_map/ppermute | solution.py:19
  20.5 38.2 %collective-permute-start.1 = (f32[2,32,180,1]{2,1,0,3:T(8,128)S(1)}, f32[2,32,180,1]{2,1,0,3:T(8,128)S(1)}, u32[]{:S(2)}, u32[]{:S(2)}) collective-permute-start(f32[2,32,180,1]{2,1,0,3:T(8,128)S(1)} %get-tuple-element.129), channel_id=1, source_target_pairs={{16,0},{32,16},{48,32},{64,48},{80,64},{96,80},{112,96},{0,112},{1... | collective-permute-start | bytes 138248 | tf_op jit(solution)/shard_map/ppermute | solution.py:20
  29.4 6.8 collective-permute-start.5
  29.5 6.7 collective-permute-start.6
  36.2 118.1 %collective-permute-start.4 = (f32[2,2,32,180]{3,2,1,0:T(8,128)S(1)}, f32[2,2,32,180]{3,2,1,0:T(8,128)S(1)}, u32[]{:S(2)}, u32[]{:S(2)}) collective-permute-start(f32[2,2,32,180]{3,2,1,0:T(8,128)S(1)} %pad_maximum_fusion.9), channel_id=1, source_target_pairs={{8,0},{9,1},{10,2},{11,3},{12,4},{13,5},{14,6},{15,7},{0,8},{1,9},... | collective-permute-start | bytes 276488 | tf_op jit(solution)/shard_map/ppermute | solution.py:28
  54.8 30.2 %collective-permute-start.8 = (f32[2,32,1,130]{3,1,2,0:T(8,128)S(1)}, f32[2,32,1,130]{3,1,2,0:T(8,128)S(1)}, u32[]{:S(2)}, u32[]{:S(2)}) collective-permute-start(f32[2,32,1,130]{3,1,2,0:T(8,128)S(1)} %copy.141), channel_id=1, source_target_pairs={{1,0},{2,1},{3,2},{4,3},{5,4},{6,5},{7,6},{8,7},{9,8},{10,9},{11,1... | collective-permute-start | bytes 99848 | tf_op jit(solution)/shard_map/ppermute | solution.py:20
  57.3 20.8 %collective-permute-start.7 = (f32[2,32,1,130]{3,1,2,0:T(8,128)S(1)}, f32[2,32,1,130]{3,1,2,0:T(8,128)S(1)}, u32[]{:S(2)}, u32[]{:S(2)}) collective-permute-start(f32[2,32,1,130]{3,1,2,0:T(8,128)S(1)} %copy.140), channel_id=1, source_target_pairs={{0,1},{1,2},{2,3},{3,4},{4,5},{5,6},{6,7},{7,8},{8,9},{9,10},{10,1... | collective-permute-start | bytes 99848 | tf_op jit(solution)/shard_map/ppermute | solution.py:19
  77.4 59.4 %collective-permute-start.3 = (f32[2,32,1,130]{3,1,2,0:T(8,128)S(1)}, f32[2,32,1,130]{3,1,2,0:T(8,128)S(1)}, u32[]{:S(2)}, u32[]{:S(2)}) collective-permute-start(f32[2,32,1,130]{3,1,2,0:T(8,128)S(1)} %copy.135), channel_id=1, source_target_pairs={{1,0},{2,1},{3,2},{4,3},{5,4},{6,5},{7,6},{8,7},{9,8},{10,9},{11,1... | collective-permute-start | bytes 99848 | tf_op jit(solution)/shard_map/ppermute | solution.py:20
  78.1 52.7 %collective-permute-start.2 = (f32[2,32,1,130]{3,1,2,0:T(8,128)S(1)}, f32[2,32,1,130]{3,1,2,0:T(8,128)S(1)}, u32[]{:S(2)}, u32[]{:S(2)}) collective-permute-start(f32[2,32,1,130]{3,1,2,0:T(8,128)S(1)} %copy.134), channel_id=1, source_target_pairs={{0,1},{1,2},{2,3},{3,4},{4,5},{5,6},{6,7},{7,8},{8,9},{9,10},{10,1... | collective-permute-start | bytes 99848 | tf_op jit(solution)/shard_map/ppermute | solution.py:19
  103.3 2.0 copy-start
  200.9 8.2 %copy-start.3 = (s32[512]{0:T(512)S(1)}, s32[512]{0:T(512)}, u32[]{:S(2)}) copy-start(s32[512]{0:T(512)} %param.25) | copy-start | bytes 6148
  200.9 86.9 %all-to-all-start = ((f32[2,32,180,128]{3,0,2,1:T(2,128)}), f32[2,32,180,128]{3,0,2,1:T(2,128)}, u32[]{:S(2)}, u32[]{:S(2)}) async-start(f32[2,32,180,128]{3,0,2,1:T(2,128)} %copy.146), calls=%async_computation | async-start | bytes 11796480 | tf_op jit(solution)/shard_map/all_to_all | solution.py:144
  300.7 14.6 %slice-start = ((s8[5898240]{0:T(1024)(128)(4,1)}), s8[4194304]{0:T(1024)(128)(4,1)S(1)}, s32[]{:S(2)}) async-start(s8[5898240]{0:T(1024)(128)(4,1)} %bitcast.101), calls=%async_computation.4 | async-start | bytes 8388608 | tf_op jit(solution)/shard_map/cond
  300.8 14.5 %slice-start.1 = ((s8[5898240]{0:T(1024)(128)(4,1)}), s8[1703936]{0:T(1024)(128)(4,1)S(1)}, s32[]{:S(2)}) async-start(s8[5898240]{0:T(1024)(128)(4,1)} %bitcast.101), calls=%async_computation.5 | async-start | bytes 3407872 | tf_op jit(solution)/shard_map/cond
  430.7 4.9 collective-permute-start.11
  434.3 6.7 collective-permute-start.10
  459.6 9.8 %collective-permute-start.13 = (f32[2,32,1,130]{3,1,2,0:T(8,128)S(1)}, f32[2,32,1,130]{3,1,2,0:T(8,128)S(1)}, u32[]{:S(2)}, u32[]{:S(2)}) collective-permute-start(f32[2,32,1,130]{3,1,2,0:T(8,128)S(1)} %copy.156), channel_id=1, source_target_pairs={{1,0},{2,1},{3,2},{4,3},{5,4},{6,5},{7,6},{8,7},{9,8},{10,9},{11,1... | collective-permute-start | bytes 99848 | tf_op jit(solution)/shard_map/ppermute | solution.py:20
  461.6 1.9 collective-permute-start.12
  462.2 23.7 %collective-permute-start.14 = (f32[2,2,32,180]{3,2,1,0:T(8,128)S(1)}, f32[2,2,32,180]{3,2,1,0:T(8,128)S(1)}, u32[]{:S(2)}, u32[]{:S(2)}) collective-permute-start(f32[2,2,32,180]{3,2,1,0:T(8,128)S(1)} %pad_maximum_fusion.10), channel_id=1, source_target_pairs={{8,0},{9,1},{10,2},{11,3},{12,4},{13,5},{14,6},{15,7},{0,8},{1,9},... | collective-permute-start | bytes 276488 | tf_op jit(solution)/shard_map/ppermute | solution.py:28
  618.5 14.6 %slice-start.2 = ((s8[5898240]{0:T(1024)(128)(4,1)}), s8[4194304]{0:T(1024)(128)(4,1)S(1)}, s32[]{:S(2)}) async-start(s8[5898240]{0:T(1024)(128)(4,1)} %bitcast.103), calls=%async_computation.6 | async-start | bytes 8388608 | tf_op jit(solution)/shard_map/cond
  618.6 14.5 %slice-start.3 = ((s8[5898240]{0:T(1024)(128)(4,1)}), s8[1703936]{0:T(1024)(128)(4,1)S(1)}, s32[]{:S(2)}) async-start(s8[5898240]{0:T(1024)(128)(4,1)} %bitcast.103), calls=%async_computation.7 | async-start | bytes 3407872 | tf_op jit(solution)/shard_map/cond
where the time goes:
time: 748 us; the launch traced here: 739 us
  blocking collectives  220 us (29%)
  local copies, waits for them, and re-layouts  207 us (28%)
  other arithmetic  152 us (20%)
  waiting for transfers between devices  72.1 us (10%)
  matrix products  51.8 us (7%)
  starting transfers between devices  33.7 us (5%)
    all_to_all x2, blocking collectives, on_device(): lax.all_to_all(spread, 'lon', split_axis=2, concat_axis=1, tiled=True)  144 us
    all_to_all x1, blocking collectives, on_device(): lax.all_to_all(advected, 'lon', split_axis=1, concat_axis=2, tiled=True)  75.6 us
    sub x2, other arithmetic, upwind(): return centre - (flux_east - flux_west) - (flux_north - flux_south)  67.7 us
    all_to_all x1, waiting for transfers between devices, on_device(): lax.all_to_all(advected, 'lon', split_axis=1, concat_axis=2, tiled=True)  62.7 us
    concatenate x6, other arithmetic, extended(): value = jnp.concatenate([before, value, after], axis=dim)  43.6 us
    cond x2, local copies, waits for them, and re-layouts, on_device(): lax.cond(is_polar, lambda inner_rows: apply_filter(inner_rows, own_cut, d...  34.4 us
    slice x6, local copies, waits for them, and re-layouts, extended(): last = lax.slice_in_dim(value, length - width, length, axis=dim)  29.2 us
    dot_general x2, matrix products, apply_filter(): jnp.einsum('pk,ilpr->ilkr', dft_table, segment_rows, precision=lax.Precis...  29 us
  transfers between devices with their start and end apart: 16, of which 5 were waited for; matrix products, arithmetic and copies ran while one was open for 22% of the time, Pallas kernels for 0%

commit v1 on v0

v1 whole, which is shorter than its diff:
```python
import functools

import jax
import jax.numpy as jnp
import ml_dtypes
import numpy as np
from jax import lax
from jax.experimental import pallas as pl
from jax.experimental.pallas import tpu as pltpu
from jax.sharding import PartitionSpec as P

KW = 256
SUBSTEPS = 2
PLANE = 8
ROUNDS = 4
MESH = pl.DeviceIdType.MESH


def split_table(table):
    high = table.astype(ml_dtypes.bfloat16)
    low = (table - high.astype(np.float64)).astype(ml_dtypes.bfloat16)
    return high, low


def dft_tables(columns, padded, inverse_rows):
    points = columns * PLANE * 2
    longitude = np.arange(PLANE * columns).reshape(PLANE, columns, 1)
    angle = (longitude * np.arange(KW) % points) * (2.0 * np.pi / points)
    table = np.concatenate([np.cos(angle), np.sin(angle)], axis=2)
    forward = np.zeros((PLANE, padded, 2 * KW))
    forward[:, :columns] = table
    inverse = np.zeros((PLANE, inverse_rows, 2 * KW))
    inverse[:, :columns] = table
    forward = forward.reshape(PLANE * padded, 2 * KW).T.copy()
    return split_table(forward) + split_table(inverse.reshape(PLANE * inverse_rows, 2 * KW))


def halves(value):
    high = value.astype(jnp.bfloat16)
    return high, (value - high.astype(jnp.float32)).astype(jnp.bfloat16)


def product(left_high, left_low, right):
    right_high, right_low = halves(right)
    dot = functools.partial(jnp.dot, preferred_element_type=jnp.float32)
    return dot(left_high, right_high) + dot(left_high, right_low) + dot(left_low, right_high)


def kernel(
    columns, padded, inverse_rows,
    thick_in, tracer_in, zonal_in, merid_in, keep, fwd_hi, fwd_lo, inv_hi, inv_lo,
    thick_out, tracer_out,
    field, zonal, merid, adv, circle, back, passed, spec, spec_in, edge, edge_in, rim, rim_in,
    in_sem, out_sem, halo_send, edge_recv, rim_recv, mig_send, mig_recv, fwd_send, fwd_recv,
    swap_send, swap_recv, ret_send, ret_recv, home_send, home_recv,
):
    band = lax.axis_index("lat")
    lon = lax.axis_index("lon")
    mine = lon % PLANE
    plane = lon - mine
    across = (lon + PLANE) % (2 * PLANE)
    east = (lon + 1) % (2 * PLANE)
    west = (lon + 2 * PLANE - 1) % (2 * PLANE)
    last_band = band // 7
    first_band = 1 - (band + 7) // 8
    helper_x = (band // 4) * 4 + 3 - band % 4
    helper_z = (band + 4) % 8
    polar = (band < 2) | (band >= 6)

    loads = [
        pltpu.make_async_copy(thick_in, field.at[:, :, 0, pl.ds(0, columns)], in_sem.at[0]),
        pltpu.make_async_copy(tracer_in, field.at[:, :, 1, pl.ds(0, columns)], in_sem.at[1]),
        pltpu.make_async_copy(zonal_in, zonal.at[:, :, pl.ds(0, columns)], in_sem.at[2]),
        pltpu.make_async_copy(merid_in, merid.at[:, :, pl.ds(0, columns)], in_sem.at[3]),
    ]
    for load in loads:
        load.start()

    barrier = pltpu.get_barrier_semaphore()
    partners = [(band, plane + (mine + step) % PLANE) for step in range(1, PLANE)]
    partners += [(band, across), (band, east), (band, west)]
    partners += [((band + 1) % 8, lon), ((band + 7) % 8, lon), (helper_x, lon), (helper_z, across)]
    for partner in partners:
        pl.semaphore_signal(barrier, inc=1, device_id=partner, device_id_type=MESH)

    row = lax.broadcasted_iota(jnp.int32, (padded, 128), 0)
    lane = lax.broadcasted_iota(jnp.int32, (padded, 128), 1)
    tail = jnp.zeros((padded - columns, 128), jnp.float32)

    def clear(index, carry):
        group, level = index // PLANE, index % PLANE
        field[group, level, 0, pl.ds(columns, padded - columns)] = tail
        field[group, level, 1, pl.ds(columns, padded - columns)] = tail
        zonal[group, level, pl.ds(columns, padded - columns)] = tail
        merid[group, level, pl.ds(columns, padded - columns)] = tail
        return carry

    lax.fori_loop(0, ROUNDS * PLANE, clear, 0)
    for load in loads:
        load.wait()
    pl.semaphore_wait(barrier, len(partners))

    def remote(src, dst, send, recv, device):
        return pltpu.make_async_remote_copy(
            src_ref=src, dst_ref=dst, send_sem=send, recv_sem=recv, device_id=device, device_id_type=MESH
        )

    def halo_copies(step, group):
        return [
            remote(rim.at[step, group, 1], rim_in.at[step, group, 0], halo_send.at[step, group, 0],
                   rim_recv.at[step, group, 0], (band, east)),
            remote(rim.at[step, group, 0], rim_in.at[step, group, 1], halo_send.at[step, group, 1],
                   rim_recv.at[step, group, 1], (band, west)),
            remote(edge.at[step, group], edge_in.at[step, group, last_band], halo_send.at[step, group, 2],
                   edge_recv.at[step, group, last_band],
                   (band + 1 - last_band, (lon + PLANE * last_band) % (2 * PLANE))),
            remote(edge.at[step, group], edge_in.at[step, group, 1 - first_band], halo_send.at[step, group, 3],
                   edge_recv.at[step, group, 1 - first_band],
                   (band - 1 + first_band, (lon + PLANE * first_band) % (2 * PLANE))),
        ]

    def halo_wait(step, group):
        for side in range(2):
            remote(rim.at[step, group, 0], rim_in.at[step, group, side], halo_send.at[step, group, 0],
                   rim_recv.at[step, group, side], (band, east)).wait_recv()
            remote(edge.at[step, group], edge_in.at[step, group, side], halo_send.at[step, group, 0],
                   edge_recv.at[step, group, side], (band, across)).wait_recv()

    def pack(step, group):
        def one(level, packed):
            values = [field[group, level, 0], field[group, level, 1]]
            if step == 0:
                values.append(merid[group, level])
            for array, value in enumerate(values):
                place = array * PLANE + level
                packed = jnp.where(lane == place, pltpu.roll(value, place, 1), packed)
                packed = jnp.where(lane == 64 + place, pltpu.roll(value, 65 + place, 1), packed)
            rows = [field.at[group, level, 0], field.at[group, level, 1]]
            if step == 0:
                rows.append(zonal.at[group, level])
            for array, ref in enumerate(rows):
                place = array * PLANE + level
                rim[step, group, 0, pl.ds(place, 1)] = ref[pl.ds(0, 1)]
                rim[step, group, 1, pl.ds(place, 1)] = ref[pl.ds(columns - 1, 1)]
            return packed

        edge[step, group] = lax.fori_loop(0, PLANE, one, jnp.zeros((padded, 128), jnp.float32))
        for copy in halo_copies(step, group):
            copy.start()

    sign_south = 1.0 - 2.0 * first_band.astype(jnp.float32)
    sign_north = 1.0 - 2.0 * last_band.astype(jnp.float32)
    south_place = 64 * (1 - first_band)
    north_place = 64 * last_band

    def advect(step, group, level):
        def eastward(value, halo):
            return jnp.where(row == columns - 1, halo, pltpu.roll(value, padded - 1, 0))

        def rims(at, place):
            return rim_in[at, group, 0, pl.ds(place, 1)], rim_in[at, group, 1, pl.ds(place, 1)]

        def northward(at, place, value, sign):
            column = pltpu.roll(edge_in[at, group, 1], 127 - north_place - place, 1)
            return jnp.where(lane == 127, column if sign is None else sign * column, pltpu.roll(value, 127, 1))

        def southward(at, place, value, sign):
            column = pltpu.roll(edge_in[at, group, 0], 128 - south_place - place, 1)
            return jnp.where(lane == 0, column if sign is None else sign * column, pltpu.roll(value, 1, 1))

        a = zonal[group, level]
        m = merid[group, level]
        west_a, east_a = rims(0, 2 * PLANE + level)
        face_east = 0.5 * (a + eastward(a, east_a))
        face_west = 0.5 * (west_a + a[0:1])
        face_north = 0.5 * (m + northward(0, 2 * PLANE + level, m, sign_north))
        face_south = 0.5 * (southward(0, 2 * PLANE + level, m, sign_south) + m)
        results = []
        for array in range(2):
            f = field[group, level, array]
            place = array * PLANE + level
            west_f, east_f = rims(step, place)
            flux_east = jnp.maximum(face_east, 0.0) * f + jnp.minimum(face_east, 0.0) * eastward(f, east_f)
            first_west = jnp.maximum(face_west, 0.0) * west_f + jnp.minimum(face_west, 0.0) * f[0:1]
            flux_west = jnp.where(row == 0, first_west, pltpu.roll(flux_east, 1, 0))
            flux_north = jnp.maximum(face_north, 0.0) * f + jnp.minimum(face_north, 0.0) * northward(step, place, f, None)
            flux_south = jnp.maximum(face_south, 0.0) * southward(step, place, f, None) + jnp.minimum(face_south, 0.0) * f
            result = f - (flux_east - flux_west) - (flux_north - flux_south)
            results.append(jnp.where(row < columns, result, 0.0))
        return results

    def mig_copy(job, level, device):
        return remote(adv.at[2 + job, level], adv.at[job, level], mig_send.at[job, level], mig_recv.at[job, level], device)

    def fwd_copy(job, level):
        return remote(adv.at[job, level], circle.at[job, mine], fwd_send.at[job, level], fwd_recv.at[job, mine],
                      (band, plane + level))

    def own_copy(job):
        return pltpu.make_async_copy(adv.at[job, mine], circle.at[job, mine], fwd_send.at[job, mine])

    def swap_copy(step, job):
        return remote(spec.at[job], spec_in.at[step, job], swap_send.at[job], swap_recv.at[job], (band, across))

    def ret_copy(job, other, target):
        return remote(back.at[job, other], target.at[job, mine], ret_send.at[job, other], ret_recv.at[job, mine],
                      (band, plane + other))

    def home_copy(job, level):
        device = (helper_x, lon) if job == 0 else (helper_z, across)
        return remote(passed.at[job, level], field.at[2 + job, level], home_send.at[job, level], home_recv.at[job, level],
                      device)

    def loop(count, body):
        def run(index, carry):
            body(index)
            return carry

        lax.fori_loop(0, count, run, 0)

    wave_row = lax.broadcasted_iota(jnp.int32, (2 * KW, 256), 0)
    parity = 1.0 - 2.0 * (wave_row % 2).astype(jnp.float32)

    for step in range(SUBSTEPS):
        for group in range(ROUNDS):
            pack(step, group)
        for group in range(ROUNDS):
            halo_wait(step, group)

        def advect_one(index, step=step):
            group = (index + 2) % ROUNDS
            level = (mine + index // ROUNDS) % PLANE
            first, second = advect(step, group, level)

            @pl.when(polar)
            def _():
                adv[group, level, 0] = first
                adv[group, level, 1] = second

                @pl.when(group == 2)
                def _():
                    mig_copy(0, level, (helper_x, lon)).start()

                @pl.when(group == 3)
                def _():
                    mig_copy(1, level, (helper_z, across)).start()

            @pl.when(jnp.logical_not(polar))
            def _():
                field[group, level, 0] = first
                field[group, level, 1] = second

                @pl.when(group < 2)
                def _():
                    mig_copy(group, level, (helper_x, lon)).wait_recv()

            @pl.when((group < 2) & (level != mine))
            def _():
                fwd_copy(group, level).start()

            @pl.when((group < 2) & (level == mine))
            def _():
                own_copy(group).start()

        loop(ROUNDS * PLANE, advect_one)

        for job in range(2):
            def arrived(index, job=job):
                source = (mine + PLANE - 1 - index) % PLANE
                remote(adv.at[job, source], circle.at[job, source], fwd_send.at[job, source], fwd_recv.at[job, source],
                       (band, plane + source)).wait_recv()

            own_copy(job).wait()
            loop(PLANE - 1, arrived)
            both = jnp.concatenate(
                [circle[job, :, 0].reshape(PLANE * padded, 128), circle[job, :, 1].reshape(PLANE * padded, 128)], axis=1
            )
            spec[job] = product(fwd_hi[...], fwd_lo[...], both)
            swap_copy(step, job).start()

        for job in range(2):
            swap_copy(step, job).wait_recv()
            weight = keep[job]
            weight = jnp.concatenate([weight, weight], axis=1)
            kept_hi, kept_lo = halves((spec[job] + parity * spec_in[step, job]) * weight)

            def give(index, job=job, kept_hi=kept_hi, kept_lo=kept_lo):
                other = (mine + 1 + index) % PLANE
                place = pl.ds(pl.multiple_of(other * inverse_rows, inverse_rows), inverse_rows)
                dot = functools.partial(jnp.dot, preferred_element_type=jnp.float32)
                value = dot(inv_hi[place], kept_hi) + dot(inv_hi[place], kept_lo) + dot(inv_lo[place], kept_hi)
                back[job, other, 0] = value[:padded, :128]
                back[job, other, 1] = value[:padded, 128:]

                @pl.when((other != mine) & polar)
                def _():
                    ret_copy(job, other, field).start()

                @pl.when((other != mine) & jnp.logical_not(polar))
                def _():
                    ret_copy(job, other, passed).start()

            loop(PLANE, give)

            @pl.when(polar)
            def _(job=job):
                field[job, mine] = back[job, mine]

            @pl.when(jnp.logical_not(polar))
            def _(job=job):
                passed[job, mine] = back[job, mine]

        for job in range(2):
            def fwd_done(index, job=job):
                fwd_copy(job, (mine + 1 + index) % PLANE).wait_send()

            loop(PLANE - 1, fwd_done)

        @pl.when(jnp.logical_not(polar))
        def _():
            for job in range(2):
                home_copy(job, mine).start()

            def forward(index):
                source = (mine + PLANE - 1 - index) % PLANE
                for job in range(2):
                    remote(back.at[job, source], passed.at[job, source], ret_send.at[job, source],
                           ret_recv.at[job, source], (band, plane + source)).wait_recv()
                    home_copy(job, source).start()

            loop(PLANE - 1, forward)

            def sent(index):
                for job in range(2):
                    home_copy(job, index).wait_send()

            loop(PLANE, sent)

        @pl.when(polar)
        def _():
            def landed(index):
                source = (mine + PLANE - 1 - index) % PLANE
                for job in range(2):
                    remote(back.at[job, source], field.at[job, source], ret_send.at[job, source],
                           ret_recv.at[job, source], (band, plane + source)).wait_recv()

            loop(PLANE - 1, landed)

            def home(index):
                for job in range(2):
                    mig_copy(job, index, (helper_x, lon)).wait_send()
                    home_copy(job, index).wait_recv()

            loop(PLANE, home)

        def ret_done(index):
            for job in range(2):
                ret_copy(job, (mine + 1 + index) % PLANE, passed).wait_send()

        loop(PLANE - 1, ret_done)
        for job in range(2):
            swap_copy(step, job).wait_send()
        for group in range(ROUNDS):
            for copy in halo_copies(step, group):
                copy.wait_send()

    stores = [
        pltpu.make_async_copy(field.at[:, :, 0, pl.ds(0, columns)], thick_out, out_sem.at[0]),
        pltpu.make_async_copy(field.at[:, :, 1, pl.ds(0, columns)], tracer_out, out_sem.at[1]),
    ]
    for store in stores:
        store.start()
    for store in stores:
        store.wait()


def kept_waves(cutoffs, source_band, lat_rows, points):
    quarter_rows = cutoffs.shape[0] // 2
    latitude = source_band * lat_rows + jnp.arange(lat_rows, dtype=jnp.int32)
    polar_index = jnp.where(latitude < quarter_rows, latitude, latitude - 2 * quarter_rows)
    slots = jnp.arange(cutoffs.shape[0], dtype=jnp.int32)
    row_cut = jnp.sum(jnp.where(polar_index[:, None] == slots[None, :], cutoffs[None, :], 0), axis=1)
    wave = jnp.arange(KW, dtype=jnp.int32)
    weight = (jnp.where(wave == 0, 1.0, 2.0) / points).astype(jnp.float32)
    kept = jnp.where(wave[:, None] < row_cut[None, :], weight[:, None], 0.0)
    return jnp.concatenate([kept, kept], axis=0)


def on_device(thickness, tracer_mass, zonal_courant, merid_courant, cutoffs):
    band = lax.axis_index("lat")
    levels, columns, lat_rows = thickness.shape
    points = columns * lax.axis_size("lon")
    padded = -(-columns // 8) * 8
    inverse_rows = -(-columns // 16) * 16
    polar = (band < 2) | (band >= 6)
    helped_x = (band // 4) * 4 + 3 - band % 4
    helped_z = (band + 4) % 8
    keep = jnp.stack(
        [
            kept_waves(cutoffs, jnp.where(polar, band, helped_x), lat_rows, points),
            kept_waves(cutoffs, jnp.where(polar, band, helped_z), lat_rows, points),
        ]
    )
    tables = [jnp.asarray(table) for table in dft_tables(columns, padded, inverse_rows)]
    shape = (ROUNDS, PLANE, columns, lat_rows)
    f32 = jnp.float32
    dma = pltpu.SemaphoreType.DMA
    piece = (2, padded, 128)
    outs = pl.pallas_call(
        functools.partial(kernel, columns, padded, inverse_rows),
        out_shape=[jax.ShapeDtypeStruct(shape, f32)] * 2,
        in_specs=[pl.BlockSpec(memory_space=pl.ANY)] * 4 + [pl.BlockSpec(memory_space=pltpu.VMEM)] * 5,
        out_specs=[pl.BlockSpec(memory_space=pl.ANY)] * 2,
        scratch_shapes=[
            pltpu.VMEM((ROUNDS, PLANE) + piece, f32),
            pltpu.VMEM((ROUNDS, PLANE, padded, 128), f32),
            pltpu.VMEM((ROUNDS, PLANE, padded, 128), f32),
            pltpu.VMEM((ROUNDS, PLANE) + piece, f32),
            pltpu.VMEM((2, PLANE) + piece, f32),
            pltpu.VMEM((2, PLANE) + piece, f32),
            pltpu.VMEM((2, PLANE) + piece, f32),
            pltpu.VMEM((2, 2 * KW, 256), f32),
            pltpu.VMEM((SUBSTEPS, 2, 2 * KW, 256), f32),
            pltpu.VMEM((SUBSTEPS, ROUNDS, padded, 128), f32),
            pltpu.VMEM((SUBSTEPS, ROUNDS, 2, padded, 128), f32),
            pltpu.VMEM((SUBSTEPS, ROUNDS, 2, 3 * PLANE, 128), f32),
            pltpu.VMEM((SUBSTEPS, ROUNDS, 2, 3 * PLANE, 128), f32),
            dma((4,)),
            dma((2,)),
            dma((SUBSTEPS, ROUNDS, 4)),
            dma((SUBSTEPS, ROUNDS, 2)),
            dma((SUBSTEPS, ROUNDS, 2)),
            dma((2, PLANE)),
            dma((2, PLANE)),
            dma((2, PLANE)),
            dma((2, PLANE)),
            dma((2,)),
            dma((2,)),
            dma((2, PLANE)),
            dma((2, PLANE)),
            dma((2, PLANE)),
            dma((2, PLANE)),
        ],
        compiler_params=pltpu.CompilerParams(
            collective_id=0, has_side_effects=True, vmem_limit_bytes=60 * 1024 * 1024
        ),
    )(
        thickness.reshape(shape),
        tracer_mass.reshape(shape),
        zonal_courant.reshape(shape),
        merid_courant.reshape(shape),
        keep,
        *tables,
    )
    return outs[0].reshape(thickness.shape), outs[1].reshape(thickness.shape)


def solution(mesh):
    placed = P(None, "lon", "lat")
    return jax.shard_map(
        on_device,
        mesh=mesh,
        in_specs=(placed, placed, placed, placed, P()),
        out_specs=(placed, placed),
        check_vma=False,
    )
```

time: 748 us -> 313 us (0.42); the launches traced: 739 us -> 313 us
  Pallas kernels: 0 us -> 288 us
  blocking collectives: 220 us -> 0 us
  local copies, waits for them, and re-layouts: 207 us -> 21.7 us
  other arithmetic: 152 us -> 1.85 us
  waiting for transfers between devices: 72.1 us -> 0 us
  matrix products: 51.8 us -> 0 us
  starting transfers between devices: 33.7 us -> 0 us
    pallas_call x0 -> x1, Pallas kernels: none -> 288 us  [on_device(): pl.pallas_call(functools.partial(kernel, columns, padded, inverse_rows),...]
    all_to_all x3 -> x0, blocking collectives: 220 us -> none  [the longest x2 144 us: on_device(): lax.all_to_all(spread, 'lon', split_axis=2, concat_axis=1, tiled=True)]
    sub x2 -> x0, other arithmetic: 67.7 us -> none  [upwind(): return centre - (flux_east - flux_west) - (flux_north - flux_south)]
    all_to_all x1 -> x0, waiting for transfers between devices: 62.7 us -> none  [on_device(): lax.all_to_all(advected, 'lon', split_axis=1, concat_axis=2, tiled=True)]
    dot_general x4 -> x0, matrix products: 51.8 us -> none  [the longest x2 29 us: apply_filter(): jnp.einsum('pk,ilpr->ilkr', dft_table, segment_rows, precision=lax.Precis...]
    concatenate x9 -> x0, other arithmetic: 47.1 us -> none  [the longest x6 43.6 us: extended(): value = jnp.concatenate([before, value, after], axis=dim)]
    slice x12 -> x0, local copies, waits for them, and re-layouts: 44.5 us -> none  [the longest x6 29.2 us: extended(): last = lax.slice_in_dim(value, length - width, length, axis=dim)]
    all_to_all x9 -> x0, local copies, waits for them, and re-layouts: 36 us -> none  [the longest x6 23.1 us: on_device(): lax.all_to_all(advected, 'lon', split_axis=1, concat_axis=2, tiled=True)]
  transfers between devices with their start and end apart: 16 -> 0, of which waited for: 5 -> 0; matrix products, arithmetic and copies ran while one was open for 22% -> 0% of each run, Pallas kernels for 0% -> 0%
where the time goes in v1:
time: 313 us
  Pallas kernels  288 us (92%)
  local copies, waits for them, and re-layouts  21.7 us (7%)
    pallas_call x1, Pallas kernels, on_device(): pl.pallas_call(functools.partial(kernel, columns, padded, inverse_rows),...  288 us
    unnamed x14, local copies, waits for them, and re-layouts  21.7 us

profile of v1, /device:TPU:1, one launch (start us, length us, event | category | flops | bytes accessed | tf_op | source)
XLA Modules:
  0.0 312.6 jit_solution(595169858643092821)
XLA Ops:
  0.7 0.9 select_reduce_fusion.1
  1.6 0.1 fusion
  1.7 0.8 pad_maximum_fusion.keep
  2.6 0.0 copy-start.1
  2.6 5.3 %copy.17 = f32[32,180,128]{2,1,0:T(8,128)} copy(f32[32,180,128]{2,0,1:T(8,128)} %param.9) | data formatting | bytes 5898240 | tf_op args[0]
  7.9 0.0 copy-done.1
  7.9 0.0 copy-start.2
  7.9 3.4 %copy.18 = f32[32,180,128]{2,1,0:T(8,128)} copy(f32[32,180,128]{2,0,1:T(8,128)S(1)} %copy-done.1) | data formatting | bytes 5898240 | tf_op args[1]
  11.3 0.0 copy-done.2
  11.3 0.0 copy-start.3
  11.3 3.4 %copy.19 = f32[32,180,128]{2,1,0:T(8,128)} copy(f32[32,180,128]{2,0,1:T(8,128)S(1)} %copy-done.2) | data formatting | bytes 5898240 | tf_op args[2]
  14.7 0.0 copy-done.3
  14.7 3.3 %copy.20 = f32[32,180,128]{2,1,0:T(8,128)} copy(f32[32,180,128]{2,0,1:T(8,128)S(1)} %copy-done.3) | data formatting | bytes 5898240 | tf_op args[3]
  18.0 288.3 %shard_map.104 = (f32[4,8,180,128]{3,2,1,0:T(8,128)}, f32[4,8,180,128]{3,2,1,0:T(8,128)}) custom-call(f32[4,8,180,128]{3,2,1,0:T(8,128)} %bitcast.10, f32[4,8,180,128]{3,2,1,0:T(8,128)} %bitcast.11, f32[4,8,180,128]{3,2,1,0:T(8,128)} %bitcast.12, f32[4,8,180,128]{3,2,1,0:T(8,128)} %bitcast.13, f32[2,512,128]{2,1,0:T(8,128)} %pad_maximum_fusion.keep, ...), custom_call_target="tpu_custom_call" | custom-call | tf_op jit(solution)/shard_map/pallas_call | solution.py:409
  306.3 0.0 copy-start
  306.3 4.2 %copy.21 = f32[32,180,128]{2,0,1:T(8,128)} copy(f32[32,180,128]{2,1,0:T(8,128)} %bitcast.15) | data formatting | bytes 5898240
  310.4 0.0 copy-done
  310.4 2.1 copy.22
  (4 shorter events, 0.0 us)
Async XLA Ops:
  2.6 5.3 %copy-start.1 = (f32[32,180,128]{2,0,1:T(8,128)S(1)}, f32[32,180,128]{2,0,1:T(8,128)}, u32[]{:S(2)}) copy-start(f32[32,180,128]{2,0,1:T(8,128)} %param.10) | copy-start | bytes 8847364
  7.9 3.4 %copy-start.2 = (f32[32,180,128]{2,0,1:T(8,128)S(1)}, f32[32,180,128]{2,0,1:T(8,128)}, u32[]{:S(2)}) copy-start(f32[32,180,128]{2,0,1:T(8,128)} %param.11) | copy-start | bytes 8847364
  11.3 3.4 %copy-start.3 = (f32[32,180,128]{2,0,1:T(8,128)S(1)}, f32[32,180,128]{2,0,1:T(8,128)}, u32[]{:S(2)}) copy-start(f32[32,180,128]{2,0,1:T(8,128)} %param.12) | copy-start | bytes 8847364
  306.3 4.2 %copy-start = (f32[4,8,180,128]{3,2,1,0:T(8,128)S(1)}, f32[4,8,180,128]{3,2,1,0:T(8,128)}, u32[]{:S(2)}) copy-start(f32[4,8,180,128]{3,2,1,0:T(8,128)} %get-tuple-element.5) | copy-start | bytes 8847364

commit v2 on v1

v2 whole, which is shorter than its diff:
```python
import functools

import jax
import jax.numpy as jnp
import ml_dtypes
import numpy as np
from jax import lax
from jax.experimental import pallas as pl
from jax.experimental.pallas import tpu as pltpu
from jax.sharding import PartitionSpec as P

KW = 256
SUBSTEPS = 2
PLANE = 8
ROUNDS = 4
CHIPS = PLANE // 2
MESH = pl.DeviceIdType.MESH


def split_table(table):
    high = table.astype(ml_dtypes.bfloat16)
    low = (table - high.astype(np.float64)).astype(ml_dtypes.bfloat16)
    return high, low


def dft_tables(columns, padded, inverse_rows):
    points = columns * PLANE * 2
    longitude = np.arange(PLANE * columns).reshape(PLANE, columns, 1)
    angle = (longitude * np.arange(KW) % points) * (2.0 * np.pi / points)
    table = np.concatenate([np.cos(angle), np.sin(angle)], axis=2)
    forward = np.zeros((PLANE, padded, 2 * KW))
    forward[:, :columns] = table
    inverse = np.zeros((PLANE, inverse_rows, 2 * KW))
    inverse[:, :columns] = table
    forward = forward.reshape(PLANE * padded, 2 * KW).T.copy()
    return split_table(forward) + split_table(inverse.reshape(PLANE * inverse_rows, 2 * KW))


def halves(value):
    high = value.astype(jnp.bfloat16)
    return high, (value - high.astype(jnp.float32)).astype(jnp.bfloat16)


def dot(left, right):
    return jnp.dot(left, right, preferred_element_type=jnp.float32)


def product(left_high, left_low, right):
    right_high, right_low = halves(right)
    return dot(left_high, right_high) + dot(left_high, right_low) + dot(left_low, right_high)


def kernel(
    columns, padded, inverse_rows,
    thick_in, tracer_in, zonal_in, merid_in, keep, fwd_hi, fwd_lo, inv_hi, inv_lo,
    thick_out, tracer_out,
    field, zonal, merid, adv, circle, back, passed, spec, spec_in, edge, edge_in, rim, rim_in,
    in_sem, out_sem, halo_send, edge_recv, rim_recv, mig_send, mig_recv, fwd_send, fwd_recv,
    swap_send, swap_recv, ret_send, ret_recv, home_send, home_recv,
):
    band = lax.axis_index("lat")
    lon = lax.axis_index("lon")
    mine = lon % PLANE
    plane = lon - mine
    chip = mine // 2
    across = (lon + PLANE) % (2 * PLANE)
    east = (lon + 1) % (2 * PLANE)
    west = (lon + 2 * PLANE - 1) % (2 * PLANE)
    last_band = band // 7
    first_band = 1 - (band + 7) // 8
    helper_x = (band // 4) * 4 + 3 - band % 4
    helper_z = (band + 4) % 8
    polar = (band < 2) | (band >= 6)
    helping = jnp.logical_not(polar)

    def loop(count, body):
        def run(index, carry):
            body(index)
            return carry

        lax.fori_loop(0, count, run, 0)

    def inner(ref, *place):
        return ref.at[place + (pl.ds(0, columns),)]

    def load_copies(group, level):
        height = group * PLANE + level
        half, slab = level // CHIPS, 2 * (level % CHIPS)
        return [
            pltpu.make_async_copy(thick_in.at[:, height], inner(field, half, group, slab), in_sem.at[group, level, 0]),
            pltpu.make_async_copy(tracer_in.at[:, height], inner(field, half, group, slab + 1), in_sem.at[group, level, 1]),
            pltpu.make_async_copy(zonal_in.at[:, height], inner(zonal, group, level), in_sem.at[group, level, 2]),
            pltpu.make_async_copy(merid_in.at[:, height], inner(merid, group, level), in_sem.at[group, level, 3]),
        ]

    def store_copies(group, level):
        height = group * PLANE + level
        half, slab = level // CHIPS, 2 * (level % CHIPS)
        return [
            pltpu.make_async_copy(inner(field, half, group, slab), thick_out.at[:, height], out_sem.at[group, level, 0]),
            pltpu.make_async_copy(inner(field, half, group, slab + 1), tracer_out.at[:, height], out_sem.at[group, level, 1]),
        ]

    def load(index):
        for copy in load_copies(index // PLANE, index % PLANE):
            copy.start()

    loop(ROUNDS * PLANE, load)

    barrier = pltpu.get_barrier_semaphore()
    partners = [(band, plane + (mine + step) % PLANE) for step in range(1, PLANE)]
    partners += [(band, across), (band, east), (band, west)]
    partners += [((band + 1) % 8, lon), ((band + 7) % 8, lon), (helper_x, lon), (helper_z, across)]
    for partner in partners:
        pl.semaphore_signal(barrier, inc=1, device_id=partner, device_id_type=MESH)

    row = lax.broadcasted_iota(jnp.int32, (padded, 128), 0)
    lane = lax.broadcasted_iota(jnp.int32, (padded, 128), 1)
    rest = pl.ds(columns, padded - columns)
    blank = jnp.zeros((padded - columns, 128), jnp.float32)

    def clear(index):
        group, level = index // PLANE, index % PLANE
        field[0, group, level, rest] = blank
        field[1, group, level, rest] = blank
        zonal[group, level, rest] = blank
        merid[group, level, rest] = blank

    loop(ROUNDS * PLANE, clear)
    pl.semaphore_wait(barrier, len(partners))

    def remote(src, dst, send, recv, device):
        return pltpu.make_async_remote_copy(
            src_ref=src, dst_ref=dst, send_sem=send, recv_sem=recv, device_id=device, device_id_type=MESH
        )

    def halo_copies(step, group):
        return [
            remote(rim.at[step, group, 1], rim_in.at[step, group, 0], halo_send.at[step, group, 0],
                   rim_recv.at[step, group, 0], (band, east)),
            remote(rim.at[step, group, 0], rim_in.at[step, group, 1], halo_send.at[step, group, 1],
                   rim_recv.at[step, group, 1], (band, west)),
            remote(edge.at[step, group], edge_in.at[step, group, last_band], halo_send.at[step, group, 2],
                   edge_recv.at[step, group, last_band],
                   (band + 1 - last_band, (lon + PLANE * last_band) % (2 * PLANE))),
            remote(edge.at[step, group], edge_in.at[step, group, 1 - first_band], halo_send.at[step, group, 3],
                   edge_recv.at[step, group, 1 - first_band],
                   (band - 1 + first_band, (lon + PLANE * first_band) % (2 * PLANE))),
        ]

    def halo_wait(step, group):
        for side in range(2):
            remote(rim.at[step, group, 0], rim_in.at[step, group, side], halo_send.at[step, group, 0],
                   rim_recv.at[step, group, side], (band, east)).wait_recv()
            remote(edge.at[step, group], edge_in.at[step, group, side], halo_send.at[step, group, 0],
                   edge_recv.at[step, group, side], (band, across)).wait_recv()

    def pack(step, group):
        def one(level, packed):
            half, slab = level // CHIPS, 2 * (level % CHIPS)
            values = [field[half, group, slab], field[half, group, slab + 1], merid[group, level]]
            for array, value in enumerate(values):
                place = array * PLANE + level
                packed = jnp.where(lane == place, pltpu.roll(value, place, 1), packed)
                packed = jnp.where(lane == 64 + place, pltpu.roll(value, 65 + place, 1), packed)
            rows = [field.at[half, group, slab], field.at[half, group, slab + 1], zonal.at[group, level]]
            for array, ref in enumerate(rows):
                place = array * PLANE + level
                rim[step, group, 0, pl.ds(place, 1)] = ref[pl.ds(0, 1)]
                rim[step, group, 1, pl.ds(place, 1)] = ref[pl.ds(columns - 1, 1)]
            return packed

        edge[step, group] = lax.fori_loop(0, PLANE, one, jnp.zeros((padded, 128), jnp.float32))
        for copy in halo_copies(step, group):
            copy.start()

    sign_south = 1.0 - 2.0 * first_band.astype(jnp.float32)
    sign_north = 1.0 - 2.0 * last_band.astype(jnp.float32)
    south_place = 64 * (1 - first_band)
    north_place = 64 * last_band

    def advect(step, group, level):
        half, slab = level // CHIPS, 2 * (level % CHIPS)

        def eastward(value, halo):
            return jnp.where(row == columns - 1, halo, pltpu.roll(value, padded - 1, 0))

        def rims(place):
            return rim_in[step, group, 0, pl.ds(place, 1)], rim_in[step, group, 1, pl.ds(place, 1)]

        def northward(place, value, sign):
            column = pltpu.roll(edge_in[step, group, 1], 127 - north_place - place, 1)
            return jnp.where(lane == 127, column if sign is None else sign * column, pltpu.roll(value, 127, 1))

        def southward(place, value, sign):
            column = pltpu.roll(edge_in[step, group, 0], 128 - south_place - place, 1)
            return jnp.where(lane == 0, column if sign is None else sign * column, pltpu.roll(value, 1, 1))

        a = zonal[group, level]
        m = merid[group, level]
        west_a, east_a = rims(2 * PLANE + level)
        face_east = 0.5 * (a + eastward(a, east_a))
        face_west = 0.5 * (west_a + a[0:1])
        face_north = 0.5 * (m + northward(2 * PLANE + level, m, sign_north))
        face_south = 0.5 * (southward(2 * PLANE + level, m, sign_south) + m)
        results = []
        for array in range(2):
            f = field[half, group, slab + array]
            place = array * PLANE + level
            west_f, east_f = rims(place)
            flux_east = jnp.maximum(face_east, 0.0) * f + jnp.minimum(face_east, 0.0) * eastward(f, east_f)
            first_west = jnp.maximum(face_west, 0.0) * west_f + jnp.minimum(face_west, 0.0) * f[0:1]
            flux_west = jnp.where(row == 0, first_west, pltpu.roll(flux_east, 1, 0))
            flux_north = jnp.maximum(face_north, 0.0) * f + jnp.minimum(face_north, 0.0) * northward(place, f, None)
            flux_south = jnp.maximum(face_south, 0.0) * southward(place, f, None) + jnp.minimum(face_south, 0.0) * f
            result = f - (flux_east - flux_west) - (flux_north - flux_south)
            results.append(jnp.where(row < columns, result, 0.0))
        return results


    def mig_copy(unit, place, device):
        pair = pl.ds(2 * place, 2)
        return remote(adv.at[1, unit, pair], adv.at[0, unit, pair], mig_send.at[unit, place], mig_recv.at[unit, place],
                      device)

    def fwd_copy(unit, slab):
        return remote(adv.at[0, unit, slab], circle.at[unit, mine], fwd_send.at[unit, slab], fwd_recv.at[unit, mine],
                      (band, plane + slab))

    def own_copy(unit):
        return pltpu.make_async_copy(adv.at[0, unit, mine], circle.at[unit, mine], fwd_send.at[unit, mine])

    def swap_copy(step, unit):
        return remote(spec.at[unit], spec_in.at[step, unit], swap_send.at[unit], swap_recv.at[unit], (band, across))

    def ret_copy(unit, other, target):
        return remote(back.at[unit, other], target.at[unit, mine], ret_send.at[unit, other], ret_recv.at[unit, mine],
                      (band, plane + other))

    def home_copy(unit, slab, device):
        return remote(passed.at[unit, slab], field.at[1, unit, slab], home_send.at[unit, slab], home_recv.at[unit, slab],
                      device)

    def send_forward(unit, slab):
        @pl.when(slab != mine)
        def _():
            fwd_copy(unit, slab).start()

        @pl.when(slab == mine)
        def _():
            own_copy(unit).start()

    def given(unit):
        def one(index):
            ret_copy(unit, (mine + 1 + index) % PLANE, passed).wait_send()

        loop(PLANE - 1, one)

    def handed(unit):
        def one(slab):
            home_copy(unit, slab, (helper_x, lon)).wait_send()

        given(unit)
        loop(PLANE, one)

    def prepare(item):
        step, unit = item // ROUNDS, item % ROUNDS

        @pl.when(step == 0)
        def _():
            def loaded(level):
                for copy in load_copies(unit, level):
                    copy.wait()

            loop(PLANE, loaded)

        @pl.when((step > 0) & polar)
        def _():
            def landed(index):
                source = (mine + PLANE - 1 - index) % PLANE
                remote(back.at[unit, source], field.at[0, unit, source], ret_send.at[unit, source],
                       ret_recv.at[unit, source], (band, plane + source)).wait_recv()

            def sent(place):
                mig_copy(unit, place, (helper_x, lon)).wait_send()

            def home(slab):
                home_copy(unit, slab, (helper_x, lon)).wait_recv()

            given(unit)
            loop(PLANE - 1, landed)
            loop(CHIPS, sent)
            loop(PLANE, home)

        @pl.when(step < SUBSTEPS)
        def _():
            pack(step, unit)

        @pl.when(step == SUBSTEPS)
        def _():
            def store(level):
                for copy in store_copies(unit, level):
                    copy.start()

            loop(PLANE, store)

    def advance(item):
        step, unit = item // ROUNDS, item % ROUNDS
        halo_wait(step, unit)

        def one(index):
            half = 1 - index % 2
            place = (chip + 1 + index // 2) % CHIPS
            slab = 2 * place
            first, second = advect(step, unit, half * CHIPS + place)

            @pl.when(helping)
            def _():
                field[half, unit, slab] = first
                field[half, unit, slab + 1] = second

            @pl.when(polar)
            def _():
                adv[half, unit, slab] = first
                adv[half, unit, slab + 1] = second

                @pl.when((half == 1) & (place < CHIPS // 2))
                def _():
                    mig_copy(unit, place, (helper_x, lon)).start()

                @pl.when((half == 1) & (place >= CHIPS // 2))
                def _():
                    mig_copy(unit, place, (helper_z, across)).start()

                @pl.when(half == 0)
                def _():
                    send_forward(unit, slab)
                    send_forward(unit, slab + 1)

        loop(PLANE, one)

    def relay(item):
        unit = item % ROUNDS

        @pl.when(item >= ROUNDS)
        def _():
            handed(unit)

        def one(index):
            place = (chip + 1 + index) % CHIPS
            mig_copy(unit, place, (helper_x, lon)).wait_recv()
            send_forward(unit, 2 * place)
            send_forward(unit, 2 * place + 1)

        loop(CHIPS, one)

    def transform(item):
        step, unit = item // ROUNDS, item % ROUNDS
        own_copy(unit).wait()

        def arrived(index):
            source = (mine + PLANE - 1 - index) % PLANE
            remote(adv.at[0, unit, source], circle.at[unit, source], fwd_send.at[unit, source],
                   fwd_recv.at[unit, source], (band, plane + source)).wait_recv()

        loop(PLANE - 1, arrived)
        spec[unit] = product(fwd_hi[...], fwd_lo[...], circle[unit].reshape(PLANE * padded, 128))
        swap_copy(step, unit).start()

    wave_row = lax.broadcasted_iota(jnp.int32, (2 * KW, 128), 0)
    parity = 1.0 - 2.0 * (wave_row % 2).astype(jnp.float32)

    def restore(item):
        step, unit = item // ROUNDS, item % ROUNDS

        def sent(index):
            fwd_copy(unit, (mine + 1 + index) % PLANE).wait_send()

        loop(PLANE - 1, sent)
        swap_copy(step, unit).wait()
        kept_hi, kept_lo = halves((spec[unit] + parity * spec_in[step, unit]) * keep[mine // CHIPS])

        def give(index):
            other = (mine + 1 + index) % PLANE
            place = pl.ds(pl.multiple_of(other * inverse_rows, inverse_rows), inverse_rows)
            value = dot(inv_hi[place], kept_hi) + dot(inv_hi[place], kept_lo) + dot(inv_lo[place], kept_hi)
            value = value[:padded]

            @pl.when(other != mine)
            def _():
                back[unit, other] = value

            @pl.when((other != mine) & polar)
            def _():
                ret_copy(unit, other, field.at[0]).start()

            @pl.when((other != mine) & helping)
            def _():
                ret_copy(unit, other, passed).start()

            @pl.when((other == mine) & polar)
            def _():
                field[0, unit, mine] = value

            @pl.when((other == mine) & helping)
            def _():
                passed[unit, mine] = value

        loop(PLANE, give)

    def send_home(item):
        unit = item % ROUNDS

        def one(index):
            slab = (mine + PLANE - index) % PLANE

            @pl.when(slab != mine)
            def _():
                remote(back.at[unit, slab], passed.at[unit, slab], ret_send.at[unit, slab],
                       ret_recv.at[unit, slab], (band, plane + slab)).wait_recv()

            @pl.when(slab < CHIPS)
            def _():
                home_copy(unit, slab, (helper_x, lon)).start()

            @pl.when(slab >= CHIPS)
            def _():
                home_copy(unit, slab, (helper_z, across)).start()

        loop(PLANE, one)

    items = SUBSTEPS * ROUNDS

    def tick(time):
        @pl.when((time < items) & polar)
        def _():
            advance(time)

        @pl.when((time >= 3) & helping)
        def _():
            send_home(time - 3)

        @pl.when((time >= 2) & (time < items + 2))
        def _():
            restore(time - 2)

        @pl.when((time >= 1) & (time < items + 1))
        def _():
            transform(time - 1)

        @pl.when((time < items) & helping)
        def _():
            relay(time)
            advance(time)

        @pl.when(polar)
        def _():
            prepare(time + 1)

        @pl.when((time < items) & helping)
        def _():
            prepare(time + ROUNDS)

    @pl.when(polar)
    def _():
        prepare(0)

    @pl.when(helping)
    def _():
        loop(ROUNDS, prepare)

    loop(items + 3, tick)

    @pl.when(helping)
    def _():
        loop(ROUNDS, handed)

    def halo_done(index):
        for copy in halo_copies(index // ROUNDS, index % ROUNDS):
            copy.wait_send()

    loop(items, halo_done)

    def stored(index):
        for copy in store_copies(index // PLANE, index % PLANE):
            copy.wait()

    loop(ROUNDS * PLANE, stored)


def kept_waves(cutoffs, source_band, lat_rows, points):
    quarter_rows = cutoffs.shape[0] // 2
    latitude = source_band * lat_rows + jnp.arange(lat_rows, dtype=jnp.int32)
    polar_index = jnp.where(latitude < quarter_rows, latitude, latitude - 2 * quarter_rows)
    slots = jnp.arange(cutoffs.shape[0], dtype=jnp.int32)
    row_cut = jnp.sum(jnp.where(polar_index[:, None] == slots[None, :], cutoffs[None, :], 0), axis=1)
    wave = jnp.arange(KW, dtype=jnp.int32)
    weight = (jnp.where(wave == 0, 1.0, 2.0) / points).astype(jnp.float32)
    kept = jnp.where(wave[:, None] < row_cut[None, :], weight[:, None], 0.0)
    return jnp.concatenate([kept, kept], axis=0)


def on_device(thickness, tracer_mass, zonal_courant, merid_courant, cutoffs):
    band = lax.axis_index("lat")
    levels, columns, lat_rows = thickness.shape
    points = columns * lax.axis_size("lon")
    padded = -(-columns // 8) * 8
    inverse_rows = -(-columns // 16) * 16
    polar = (band < 2) | (band >= 6)
    helped_x = (band // 4) * 4 + 3 - band % 4
    helped_z = (band + 4) % 8
    keep = jnp.stack(
        [
            kept_waves(cutoffs, jnp.where(polar, band, helped_x), lat_rows, points),
            kept_waves(cutoffs, jnp.where(polar, band, helped_z), lat_rows, points),
        ]
    )
    tables = [jnp.asarray(table) for table in dft_tables(columns, padded, inverse_rows)]
    shape = (columns, levels, lat_rows)
    f32 = jnp.float32
    dma = pltpu.SemaphoreType.DMA
    piece = (PLANE, padded, 128)
    outs = pl.pallas_call(
        functools.partial(kernel, columns, padded, inverse_rows),
        out_shape=[jax.ShapeDtypeStruct(shape, f32)] * 2,
        in_specs=[pl.BlockSpec(memory_space=pl.ANY)] * 4 + [pl.BlockSpec(memory_space=pltpu.VMEM)] * 5,
        out_specs=[pl.BlockSpec(memory_space=pl.ANY)] * 2,
        scratch_shapes=[
            pltpu.VMEM((2, ROUNDS) + piece, f32),
            pltpu.VMEM((ROUNDS,) + piece, f32),
            pltpu.VMEM((ROUNDS,) + piece, f32),
            pltpu.VMEM((2, ROUNDS) + piece, f32),
            pltpu.VMEM((ROUNDS,) + piece, f32),
            pltpu.VMEM((ROUNDS,) + piece, f32),
            pltpu.VMEM((ROUNDS,) + piece, f32),
            pltpu.VMEM((ROUNDS, 2 * KW, 128), f32),
            pltpu.VMEM((SUBSTEPS, ROUNDS, 2 * KW, 128), f32),
            pltpu.VMEM((SUBSTEPS, ROUNDS, padded, 128), f32),
            pltpu.VMEM((SUBSTEPS, ROUNDS, 2, padded, 128), f32),
            pltpu.VMEM((SUBSTEPS, ROUNDS, 2, 3 * PLANE, 128), f32),
            pltpu.VMEM((SUBSTEPS, ROUNDS, 2, 3 * PLANE, 128), f32),
            dma((ROUNDS, PLANE, 4)),
            dma((ROUNDS, PLANE, 2)),
            dma((SUBSTEPS, ROUNDS, 4)),
            dma((SUBSTEPS, ROUNDS, 2)),
            dma((SUBSTEPS, ROUNDS, 2)),
            dma((ROUNDS, CHIPS)),
            dma((ROUNDS, CHIPS)),
            dma((ROUNDS, PLANE)),
            dma((ROUNDS, PLANE)),
            dma((ROUNDS,)),
            dma((ROUNDS,)),
            dma((ROUNDS, PLANE)),
            dma((ROUNDS, PLANE)),
            dma((ROUNDS, PLANE)),
            dma((ROUNDS, PLANE)),
        ],
        compiler_params=pltpu.CompilerParams(
            collective_id=0, has_side_effects=True, vmem_limit_bytes=60 * 1024 * 1024
        ),
    )(
        jnp.transpose(thickness, (1, 0, 2)),
        jnp.transpose(tracer_mass, (1, 0, 2)),
        jnp.transpose(zonal_courant, (1, 0, 2)),
        jnp.transpose(merid_courant, (1, 0, 2)),
        keep,
        *tables,
    )
    return tuple(jnp.transpose(out, (1, 0, 2)) for out in outs)


def solution(mesh):
    placed = P(None, "lon", "lat")
    return jax.shard_map(
        on_device,
        mesh=mesh,
        in_specs=(placed, placed, placed, placed, P()),
        out_specs=(placed, placed),
        check_vma=False,
    )
```

time: 313 us -> 209 us (0.67)
  Pallas kernels: 288 us -> 201 us
  local copies, waits for them, and re-layouts: 21.7 us -> 5.47 us
    pallas_call x1, Pallas kernels: 288 us -> 201 us  [on_device(): pl.pallas_call(functools.partial(kernel, columns, padded, inverse_rows),...]
    unnamed x14 -> x4, local copies, waits for them, and re-layouts: 21.7 us -> 5.47 us
where the time goes in v2:
time: 209 us
  Pallas kernels  201 us (96%)
  local copies, waits for them, and re-layouts  5.47 us (3%)
    pallas_call x1, Pallas kernels, on_device(): pl.pallas_call(functools.partial(kernel, columns, padded, inverse_rows),...  201 us
    unnamed x4, local copies, waits for them, and re-layouts  5.47 us

profile of v2, /device:TPU:1, one launch (start us, length us, event | category | flops | bytes accessed | tf_op | source)
XLA Modules:
  0.0 209.2 jit_solution(11462242334640129611)
XLA Ops:
  0.7 0.9 select_reduce_fusion.1
  1.6 0.1 fusion
  1.7 0.8 pad_maximum_fusion.keep
  2.6 201.1 %shard_map.104 = (f32[180,32,128]{2,1,0:T(8,128)}, f32[180,32,128]{2,1,0:T(8,128)}) custom-call(f32[180,32,128]{2,1,0:T(8,128)} %bitcast.10, f32[180,32,128]{2,1,0:T(8,128)} %bitcast.11, f32[180,32,128]{2,1,0:T(8,128)} %bitcast.12, f32[180,32,128]{2,1,0:T(8,128)} %bitcast.13, f32[2,512,128]{2,1,0:T(8,128)} %pad_maximum_fusion.keep, ...), custom_call_target="tpu_custom_call" | custom-call | tf_op jit(solution)/shard_map/pallas_call | solution.py:523
  203.7 0.0 copy-start
  203.7 3.9 %copy.13 = f32[32,180,128]{2,0,1:T(8,128)} copy(f32[32,180,128]{2,0,1:T(8,128)} %bitcast.15) | data formatting | bytes 5898240
  207.6 0.0 copy-done
  207.6 1.6 copy.14
  (4 shorter events, 0.0 us)
Async XLA Ops:
  203.7 3.9 %copy-start = (f32[180,32,128]{2,1,0:T(8,128)S(1)}, f32[180,32,128]{2,1,0:T(8,128)}, u32[]{:S(2)}) copy-start(f32[180,32,128]{2,1,0:T(8,128)} %get-tuple-element.5) | copy-start | bytes 8847364

commit v3 on v2

--- a/solution.py
+++ b/solution.py
@@ -52,9 +52,10 @@
 
 def kernel(
     columns, padded, inverse_rows,
-    thick_in, tracer_in, zonal_in, merid_in, keep, fwd_hi, fwd_lo, inv_hi, inv_lo,
+    thick_in, tracer_in, zonal_in, merid_in, keep, fwd_hi_in, fwd_lo_in, inv_hi_in, inv_lo_in,
     thick_out, tracer_out,
-    field, zonal, merid, adv, circle, back, passed, spec, spec_in, edge, edge_in, rim, rim_in,
+    fwd_hi, fwd_lo, inv_hi, inv_lo, table_sem,
+    field, zonal, merid, adv, circle, back, passed, spec, spec_in, halo, edge, edge_in, rim, rim_in,
     in_sem, out_sem, halo_send, edge_recv, rim_recv, mig_send, mig_recv, fwd_send, fwd_recv,
     swap_send, swap_recv, ret_send, ret_recv, home_send, home_recv,
 ):
@@ -106,6 +107,14 @@
             copy.start()
 
     loop(ROUNDS * PLANE, load)
+    tables = [
+        pltpu.make_async_copy(fwd_hi_in, fwd_hi, table_sem.at[0]),
+        pltpu.make_async_copy(fwd_lo_in, fwd_lo, table_sem.at[1]),
+        pltpu.make_async_copy(inv_hi_in, inv_hi, table_sem.at[2]),
+        pltpu.make_async_copy(inv_lo_in, inv_lo, table_sem.at[3]),
+    ]
+    for table in tables:
+        table.start()
 
     barrier = pltpu.get_barrier_semaphore()
     partners = [(band, plane + (mine + step) % PLANE) for step in range(1, PLANE)]
@@ -140,10 +149,10 @@
                    rim_recv.at[step, group, 0], (band, east)),
             remote(rim.at[step, group, 0], rim_in.at[step, group, 1], halo_send.at[step, group, 1],
                    rim_recv.at[step, group, 1], (band, west)),
-            remote(edge.at[step, group], edge_in.at[step, group, last_band], halo_send.at[step, group, 2],
+            remote(edge.at[step, group, pl.ds(64, 3 * PLANE)], edge_in.at[step, group, last_band], halo_send.at[step, group, 2],
                    edge_recv.at[step, group, last_band],
                    (band + 1 - last_band, (lon + PLANE * last_band) % (2 * PLANE))),
-            remote(edge.at[step, group], edge_in.at[step, group, 1 - first_band], halo_send.at[step, group, 3],
+            remote(edge.at[step, group, pl.ds(0, 3 * PLANE)], edge_in.at[step, group, 1 - first_band], halo_send.at[step, group, 3],
                    edge_recv.at[step, group, 1 - first_band],
                    (band - 1 + first_band, (lon + PLANE * first_band) % (2 * PLANE))),
         ]
@@ -152,7 +161,7 @@
         for side in range(2):
             remote(rim.at[step, group, 0], rim_in.at[step, group, side], halo_send.at[step, group, 0],
                    rim_recv.at[step, group, side], (band, east)).wait_recv()
-            remote(edge.at[step, group], edge_in.at[step, group, side], halo_send.at[step, group, 0],
+            remote(edge.at[step, group, pl.ds(0, 3 * PLANE)], edge_in.at[step, group, side], halo_send.at[step, group, 0],
                    edge_recv.at[step, group, side], (band, across)).wait_recv()
 
     def pack(step, group):
@@ -170,30 +179,29 @@
                 rim[step, group, 1, pl.ds(place, 1)] = ref[pl.ds(columns - 1, 1)]
             return packed
 
-        edge[step, group] = lax.fori_loop(0, PLANE, one, jnp.zeros((padded, 128), jnp.float32))
+        packed = lax.fori_loop(0, PLANE, one, jnp.zeros((padded, 128), jnp.float32))
+        edge[step, group] = jnp.transpose(packed)
         for copy in halo_copies(step, group):
             copy.start()
 
     sign_south = 1.0 - 2.0 * first_band.astype(jnp.float32)
     sign_north = 1.0 - 2.0 * last_band.astype(jnp.float32)
-    south_place = 64 * (1 - first_band)
-    north_place = 64 * last_band
 
     def advect(step, group, level):
         half, slab = level // CHIPS, 2 * (level % CHIPS)
 
-        def eastward(value, halo):
-            return jnp.where(row == columns - 1, halo, pltpu.roll(value, padded - 1, 0))
+        def eastward(value, rim_row):
+            return jnp.where(row == columns - 1, rim_row, pltpu.roll(value, padded - 1, 0))
 
         def rims(place):
             return rim_in[step, group, 0, pl.ds(place, 1)], rim_in[step, group, 1, pl.ds(place, 1)]
 
         def northward(place, value, sign):
-            column = pltpu.roll(edge_in[step, group, 1], 127 - north_place - place, 1)
+            column = pltpu.roll(halo[1], 127 - place, 1)
             return jnp.where(lane == 127, column if sign is None else sign * column, pltpu.roll(value, 127, 1))
 
         def southward(place, value, sign):
-            column = pltpu.roll(edge_in[step, group, 0], 128 - south_place - place, 1)
+            column = pltpu.roll(halo[0], 128 - place, 1)
             return jnp.where(lane == 0, column if sign is None else sign * column, pltpu.roll(value, 1, 1))
 
         a = zonal[group, level]
@@ -307,6 +315,9 @@
     def advance(item):
         step, unit = item // ROUNDS, item % ROUNDS
         halo_wait(step, unit)
+        unused = jnp.zeros((128 - 3 * PLANE, padded), jnp.float32)
+        for side in range(2):
+            halo[side] = jnp.transpose(jnp.concatenate([edge_in[step, unit, side], unused], axis=0))
 
         def one(index):
             half = 1 - index % 2
@@ -356,6 +367,11 @@
 
     def transform(item):
         step, unit = item // ROUNDS, item % ROUNDS
+        @pl.when(item == 0)
+        def _():
+            for table in tables:
+                table.wait()
+
         own_copy(unit).wait()
 
         def arrived(index):
@@ -436,6 +452,14 @@
         def _():
             advance(time)
 
+        @pl.when((time + 2 < ROUNDS) & polar)
+        def _():
+            prepare(time + 2)
+
+        @pl.when((time + 1 >= ROUNDS) & polar)
+        def _():
+            prepare(time + 1)
+
         @pl.when((time >= 3) & helping)
         def _():
             send_home(time - 3)
@@ -453,17 +477,13 @@
             relay(time)
             advance(time)
 
-        @pl.when(polar)
-        def _():
-            prepare(time + 1)
-
         @pl.when((time < items) & helping)
         def _():
             prepare(time + ROUNDS)
 
     @pl.when(polar)
     def _():
-        prepare(0)
+        loop(2, prepare)
 
     @pl.when(helping)
     def _():
@@ -523,9 +543,13 @@
     outs = pl.pallas_call(
         functools.partial(kernel, columns, padded, inverse_rows),
         out_shape=[jax.ShapeDtypeStruct(shape, f32)] * 2,
-        in_specs=[pl.BlockSpec(memory_space=pl.ANY)] * 4 + [pl.BlockSpec(memory_space=pltpu.VMEM)] * 5,
+        in_specs=[pl.BlockSpec(memory_space=pl.ANY)] * 4
+        + [pl.BlockSpec(memory_space=pltpu.VMEM)]
+        + [pl.BlockSpec(memory_space=pl.ANY)] * 4,
         out_specs=[pl.BlockSpec(memory_space=pl.ANY)] * 2,
-        scratch_shapes=[
+        scratch_shapes=[pltpu.VMEM(table.shape, table.dtype) for table in tables]
+        + [
+            dma((4,)),
             pltpu.VMEM((2, ROUNDS) + piece, f32),
             pltpu.VMEM((ROUNDS,) + piece, f32),
             pltpu.VMEM((ROUNDS,) + piece, f32),
@@ -535,8 +559,9 @@
             pltpu.VMEM((ROUNDS,) + piece, f32),
             pltpu.VMEM((ROUNDS, 2 * KW, 128), f32),
             pltpu.VMEM((SUBSTEPS, ROUNDS, 2 * KW, 128), f32),
-            pltpu.VMEM((SUBSTEPS, ROUNDS, padded, 128), f32),
-            pltpu.VMEM((SUBSTEPS, ROUNDS, 2, padded, 128), f32),
+            pltpu.VMEM((2, padded, 128), f32),
+            pltpu.VMEM((SUBSTEPS, ROUNDS, 128, padded), f32),
+            pltpu.VMEM((SUBSTEPS, ROUNDS, 2, 3 * PLANE, padded), f32),
             pltpu.VMEM((SUBSTEPS, ROUNDS, 2, 3 * PLANE, 128), f32),
             pltpu.VMEM((SUBSTEPS, ROUNDS, 2, 3 * PLANE, 128), f32),
             dma((ROUNDS, PLANE, 4)),

time: 209 us -> 186 us (0.89)
  Pallas kernels: 201 us -> 177 us
    pallas_call x1, Pallas kernels: 201 us -> 177 us  [on_device(): pl.pallas_call(functools.partial(kernel, columns, padded, inverse_rows),...]
where the time goes in v3:
time: 186 us
  Pallas kernels  177 us (95%)
  local copies, waits for them, and re-layouts  5.47 us (3%)
    pallas_call x1, Pallas kernels, on_device(): pl.pallas_call(functools.partial(kernel, columns, padded, inverse_rows),...  177 us
    unnamed x4, local copies, waits for them, and re-layouts  5.47 us

profile of v3, /device:TPU:1, one launch (start us, length us, event | category | flops | bytes accessed | tf_op | source)
XLA Modules:
  0.0 185.5 jit_solution(13811758549995177926)
XLA Ops:
  0.7 0.9 select_reduce_fusion.1
  1.6 0.1 fusion
  1.7 0.8 pad_maximum_fusion.keep
  2.6 177.5 %shard_map.104 = (f32[180,32,128]{2,1,0:T(8,128)}, f32[180,32,128]{2,1,0:T(8,128)}) custom-call(f32[180,32,128]{2,1,0:T(8,128)} %bitcast.10, f32[180,32,128]{2,1,0:T(8,128)} %bitcast.11, f32[180,32,128]{2,1,0:T(8,128)} %bitcast.12, f32[180,32,128]{2,1,0:T(8,128)} %bitcast.13, f32[2,512,128]{2,1,0:T(8,128)} %pad_maximum_fusion.keep, ...), custom_call_target="tpu_custom_call" | custom-call | tf_op jit(solution)/shard_map/pallas_call | solution.py:543
  180.1 0.0 copy-start
  180.1 3.9 %copy.13 = f32[32,180,128]{2,0,1:T(8,128)} copy(f32[32,180,128]{2,0,1:T(8,128)} %bitcast.15) | data formatting | bytes 5898240
  183.9 0.0 copy-done
  183.9 1.6 copy.14
  (4 shorter events, 0.0 us)
Async XLA Ops:
  180.1 3.9 %copy-start = (f32[180,32,128]{2,1,0:T(8,128)S(1)}, f32[180,32,128]{2,1,0:T(8,128)}, u32[]{:S(2)}) copy-start(f32[180,32,128]{2,1,0:T(8,128)} %get-tuple-element.5) | copy-start | bytes 8847364

commit v4 on v3

--- a/solution.py
+++ b/solution.py
@@ -52,7 +52,7 @@
 
 def kernel(
     columns, padded, inverse_rows,
-    thick_in, tracer_in, zonal_in, merid_in, keep, fwd_hi_in, fwd_lo_in, inv_hi_in, inv_lo_in,
+    thick_in, tracer_in, zonal_in, merid_in, cuts, fwd_hi_in, fwd_lo_in, inv_hi_in, inv_lo_in,
     thick_out, tracer_out,
     fwd_hi, fwd_lo, inv_hi, inv_lo, table_sem,
     field, zonal, merid, adv, circle, back, passed, spec, spec_in, halo, edge, edge_in, rim, rim_in,
@@ -133,6 +133,7 @@
         field[0, group, level, rest] = blank
         field[1, group, level, rest] = blank
         zonal[group, level, rest] = blank
+        circle[group, level, rest] = blank
         merid[group, level, rest] = blank
 
     loop(ROUNDS * PLANE, clear)
@@ -172,8 +173,8 @@
                 place = array * PLANE + level
                 packed = jnp.where(lane == place, pltpu.roll(value, place, 1), packed)
                 packed = jnp.where(lane == 64 + place, pltpu.roll(value, 65 + place, 1), packed)
-            rows = [field.at[half, group, slab], field.at[half, group, slab + 1], zonal.at[group, level]]
-            for array, ref in enumerate(rows):
+            outer = [field.at[half, group, slab], field.at[half, group, slab + 1], zonal.at[group, level]]
+            for array, ref in enumerate(outer):
                 place = array * PLANE + level
                 rim[step, group, 0, pl.ds(place, 1)] = ref[pl.ds(0, 1)]
                 rim[step, group, 1, pl.ds(place, 1)] = ref[pl.ds(columns - 1, 1)]
@@ -226,27 +227,29 @@
         return results
 
 
+    rows = pl.ds(0, columns)
+
     def mig_copy(unit, place, device):
         pair = pl.ds(2 * place, 2)
-        return remote(adv.at[1, unit, pair], adv.at[0, unit, pair], mig_send.at[unit, place], mig_recv.at[unit, place],
+        return remote(adv.at[1, unit, pair, rows], adv.at[0, unit, pair, rows], mig_send.at[unit, place], mig_recv.at[unit, place],
                       device)
 
     def fwd_copy(unit, slab):
-        return remote(adv.at[0, unit, slab], circle.at[unit, mine], fwd_send.at[unit, slab], fwd_recv.at[unit, mine],
+        return remote(adv.at[0, unit, slab, rows], circle.at[unit, mine, rows], fwd_send.at[unit, slab], fwd_recv.at[unit, mine],
                       (band, plane + slab))
 
     def own_copy(unit):
-        return pltpu.make_async_copy(adv.at[0, unit, mine], circle.at[unit, mine], fwd_send.at[unit, mine])
+        return pltpu.make_async_copy(adv.at[0, unit, mine, rows], circle.at[unit, mine, rows], fwd_send.at[unit, mine])
 
     def swap_copy(step, unit):
         return remote(spec.at[unit], spec_in.at[step, unit], swap_send.at[unit], swap_recv.at[unit], (band, across))
 
     def ret_copy(unit, other, target):
-        return remote(back.at[unit, other], target.at[unit, mine], ret_send.at[unit, other], ret_recv.at[unit, mine],
+        return remote(back.at[unit, other, rows], target.at[unit, mine, rows], ret_send.at[unit, other], ret_recv.at[unit, mine],
                       (band, plane + other))
 
     def home_copy(unit, slab, device):
-        return remote(passed.at[unit, slab], field.at[1, unit, slab], home_send.at[unit, slab], home_recv.at[unit, slab],
+        return remote(passed.at[unit, slab, rows], field.at[1, unit, slab, rows], home_send.at[unit, slab], home_recv.at[unit, slab],
                       device)
 
     def send_forward(unit, slab):
@@ -286,7 +289,7 @@
         def _():
             def landed(index):
                 source = (mine + PLANE - 1 - index) % PLANE
-                remote(back.at[unit, source], field.at[0, unit, source], ret_send.at[unit, source],
+                remote(back.at[unit, source, rows], field.at[0, unit, source, rows], ret_send.at[unit, source],
                        ret_recv.at[unit, source], (band, plane + source)).wait_recv()
 
             def sent(place):
@@ -376,7 +379,7 @@
 
         def arrived(index):
             source = (mine + PLANE - 1 - index) % PLANE
-            remote(adv.at[0, unit, source], circle.at[unit, source], fwd_send.at[unit, source],
+            remote(adv.at[0, unit, source, rows], circle.at[unit, source, rows], fwd_send.at[unit, source],
                    fwd_recv.at[unit, source], (band, plane + source)).wait_recv()
 
         loop(PLANE - 1, arrived)
@@ -385,6 +388,9 @@
 
     wave_row = lax.broadcasted_iota(jnp.int32, (2 * KW, 128), 0)
     parity = 1.0 - 2.0 * (wave_row % 2).astype(jnp.float32)
+    wave = wave_row % KW
+    wave_weight = jnp.where(wave == 0, 1.0 / (2 * PLANE * columns), 2.0 / (2 * PLANE * columns))
+    source_band = jnp.where(polar, band, jnp.where(mine < CHIPS, helper_x, helper_z))
 
     def restore(item):
         step, unit = item // ROUNDS, item % ROUNDS
@@ -394,7 +400,8 @@
 
         loop(PLANE - 1, sent)
         swap_copy(step, unit).wait()
-        kept_hi, kept_lo = halves((spec[unit] + parity * spec_in[step, unit]) * keep[mine // CHIPS])
+        kept = jnp.where(wave < cuts[pl.ds(source_band % 4, 1)], wave_weight, 0.0)
+        kept_hi, kept_lo = halves((spec[unit] + parity * spec_in[step, unit]) * kept)
 
         def give(index):
             other = (mine + 1 + index) % PLANE
@@ -432,7 +439,7 @@
 
             @pl.when(slab != mine)
             def _():
-                remote(back.at[unit, slab], passed.at[unit, slab], ret_send.at[unit, slab],
+                remote(back.at[unit, slab, rows], passed.at[unit, slab, rows], ret_send.at[unit, slab],
                        ret_recv.at[unit, slab], (band, plane + slab)).wait_recv()
 
             @pl.when(slab < CHIPS)
@@ -456,7 +463,7 @@
         def _():
             prepare(time + 2)
 
-        @pl.when((time + 1 >= ROUNDS) & polar)
+        @pl.when((time + 1 >= ROUNDS) & (time < items) & polar)
         def _():
             prepare(time + 1)
 
@@ -471,6 +478,10 @@
         @pl.when((time >= 1) & (time < items + 1))
         def _():
             transform(time - 1)
+
+        @pl.when((time >= items) & polar)
+        def _():
+            prepare(time + 1)
 
         @pl.when((time < items) & helping)
         def _():
@@ -508,33 +519,10 @@
     loop(ROUNDS * PLANE, stored)
 
 
-def kept_waves(cutoffs, source_band, lat_rows, points):
-    quarter_rows = cutoffs.shape[0] // 2
-    latitude = source_band * lat_rows + jnp.arange(lat_rows, dtype=jnp.int32)
-    polar_index = jnp.where(latitude < quarter_rows, latitude, latitude - 2 * quarter_rows)
-    slots = jnp.arange(cutoffs.shape[0], dtype=jnp.int32)
-    row_cut = jnp.sum(jnp.where(polar_index[:, None] == slots[None, :], cutoffs[None, :], 0), axis=1)
-    wave = jnp.arange(KW, dtype=jnp.int32)
-    weight = (jnp.where(wave == 0, 1.0, 2.0) / points).astype(jnp.float32)
-    kept = jnp.where(wave[:, None] < row_cut[None, :], weight[:, None], 0.0)
-    return jnp.concatenate([kept, kept], axis=0)
-
-
 def on_device(thickness, tracer_mass, zonal_courant, merid_courant, cutoffs):
-    band = lax.axis_index("lat")
     levels, columns, lat_rows = thickness.shape
-    points = columns * lax.axis_size("lon")
     padded = -(-columns // 8) * 8
     inverse_rows = -(-columns // 16) * 16
-    polar = (band < 2) | (band >= 6)
-    helped_x = (band // 4) * 4 + 3 - band % 4
-    helped_z = (band + 4) % 8
-    keep = jnp.stack(
-        [
-            kept_waves(cutoffs, jnp.where(polar, band, helped_x), lat_rows, points),
-            kept_waves(cutoffs, jnp.where(polar, band, helped_z), lat_rows, points),
-        ]
-    )
     tables = [jnp.asarray(table) for table in dft_tables(columns, padded, inverse_rows)]
     shape = (columns, levels, lat_rows)
     f32 = jnp.float32
@@ -588,7 +576,7 @@
         jnp.transpose(tracer_mass, (1, 0, 2)),
         jnp.transpose(zonal_courant, (1, 0, 2)),
         jnp.transpose(merid_courant, (1, 0, 2)),
-        keep,
+        cutoffs.reshape(-1, lat_rows),
         *tables,
     )
     return tuple(jnp.transpose(out, (1, 0, 2)) for out in outs)

time: 186 us -> 180 us (0.968)
  Pallas kernels: 177 us -> 173 us
    pallas_call x1, Pallas kernels: 177 us -> 173 us  [on_device(): pl.pallas_call(functools.partial(kernel, columns, padded, inverse_rows),...]
where the time goes in v4:
time: 180 us
  Pallas kernels  173 us (96%)
  local copies, waits for them, and re-layouts  5.47 us (3%)
    pallas_call x1, Pallas kernels, on_device(): pl.pallas_call(functools.partial(kernel, columns, padded, inverse_rows),...  173 us
    unnamed x4, local copies, waits for them, and re-layouts  5.47 us

profile of v4, /device:TPU:1, one launch (start us, length us, event | category | flops | bytes accessed | tf_op | source)
XLA Modules:
  0.0 179.5 jit_solution(14283958862188807272)
XLA Ops:
  0.6 173.4 %shard_map.104 = (f32[180,32,128]{2,1,0:T(8,128)}, f32[180,32,128]{2,1,0:T(8,128)}) custom-call(f32[180,32,128]{2,1,0:T(8,128)} %bitcast.7, f32[180,32,128]{2,1,0:T(8,128)} %bitcast.8, f32[180,32,128]{2,1,0:T(8,128)} %bitcast.9, f32[180,32,128]{2,1,0:T(8,128)} %bitcast.10, s32[4,128]{1,0:T(4,128)} %bitcast.13, bf16[512,1472]{1,0:T(8,128)(2,1)} %constant.8.clone.fwd_hi_in, ...), custom_call_target="tpu_custom_call" | custom-call | tf_op jit(solution)/shard_map/pallas_call | solution.py:531
  174.1 0.0 copy-start
  174.1 3.9 %copy.13 = f32[32,180,128]{2,0,1:T(8,128)} copy(f32[32,180,128]{2,0,1:T(8,128)} %bitcast.12) | data formatting | bytes 5898240
  177.9 0.0 copy-done
  177.9 1.6 copy.14
Async XLA Ops:
  174.1 3.9 %copy-start = (f32[180,32,128]{2,1,0:T(8,128)S(1)}, f32[180,32,128]{2,1,0:T(8,128)}, u32[]{:S(2)}) copy-start(f32[180,32,128]{2,1,0:T(8,128)} %get-tuple-element.5) | copy-start | bytes 8847364

commit v5 on v4

--- a/solution.py
+++ b/solution.py
@@ -53,7 +53,7 @@
 def kernel(
     columns, padded, inverse_rows,
     thick_in, tracer_in, zonal_in, merid_in, cuts, fwd_hi_in, fwd_lo_in, inv_hi_in, inv_lo_in,
-    thick_out, tracer_out,
+    out,
     fwd_hi, fwd_lo, inv_hi, inv_lo, table_sem,
     field, zonal, merid, adv, circle, back, passed, spec, spec_in, halo, edge, edge_in, rim, rim_in,
     in_sem, out_sem, halo_send, edge_recv, rim_recv, mig_send, mig_recv, fwd_send, fwd_recv,
@@ -98,8 +98,8 @@
         height = group * PLANE + level
         half, slab = level // CHIPS, 2 * (level % CHIPS)
         return [
-            pltpu.make_async_copy(inner(field, half, group, slab), thick_out.at[:, height], out_sem.at[group, level, 0]),
-            pltpu.make_async_copy(inner(field, half, group, slab + 1), tracer_out.at[:, height], out_sem.at[group, level, 1]),
+            pltpu.make_async_copy(inner(field, half, group, slab), out.at[0, :, height], out_sem.at[group, level, 0]),
+            pltpu.make_async_copy(inner(field, half, group, slab + 1), out.at[1, :, height], out_sem.at[group, level, 1]),
         ]
 
     def load(index):
@@ -530,11 +530,11 @@
     piece = (PLANE, padded, 128)
     outs = pl.pallas_call(
         functools.partial(kernel, columns, padded, inverse_rows),
-        out_shape=[jax.ShapeDtypeStruct(shape, f32)] * 2,
+        out_shape=jax.ShapeDtypeStruct((2,) + shape, f32),
         in_specs=[pl.BlockSpec(memory_space=pl.ANY)] * 4
         + [pl.BlockSpec(memory_space=pltpu.VMEM)]
         + [pl.BlockSpec(memory_space=pl.ANY)] * 4,
-        out_specs=[pl.BlockSpec(memory_space=pl.ANY)] * 2,
+        out_specs=pl.BlockSpec(memory_space=pl.ANY),
         scratch_shapes=[pltpu.VMEM(table.shape, table.dtype) for table in tables]
         + [
             dma((4,)),

time: 180 us -> 180 us (level)
    transpose x0 -> x1, local copies, waits for them, and re-layouts: none -> 5.96 us  [on_device(): return tuple((jnp.transpose(out, (1, 0, 2)) for out in outs))]
    unnamed x4 -> x0, local copies, waits for them, and re-layouts: 5.47 us -> none
where the time goes in v5:
time: 180 us
  Pallas kernels  173 us (96%)
  local copies, waits for them, and re-layouts  5.96 us (3%)
    pallas_call x1, Pallas kernels, on_device(): pl.pallas_call(functools.partial(kernel, columns, padded, inverse_rows),...  173 us
    transpose x1, local copies, waits for them, and re-layouts, on_device(): return tuple((jnp.transpose(out, (1, 0, 2)) for out in outs))  5.96 us

profile of v5, /device:TPU:1, one launch (start us, length us, event | category | flops | bytes accessed | tf_op | source)
XLA Modules:
  0.0 180.0 jit_solution(15558522951728392863)
XLA Ops:
  0.6 173.4 %shard_map.104 = f32[2,180,32,128]{3,2,1,0:T(8,128)} custom-call(f32[180,32,128]{2,1,0:T(8,128)} %bitcast.13, f32[180,32,128]{2,1,0:T(8,128)} %bitcast.14, f32[180,32,128]{2,1,0:T(8,128)} %bitcast.15, f32[180,32,128]{2,1,0:T(8,128)} %bitcast.16, s32[4,128]{1,0:T(4,128)} %bitcast.17, bf16[512,1472]{1,0:T(8,128)(2,1)} %constant.8.clone.fwd_hi_in, ...), custom_call_target="tpu_custom_call" | custom-call | tf_op jit(solution)/shard_map/pallas_call | solution.py:531
  174.1 6.0 %slice_bitcast_fusion = (f32[32,180,128]{2,0,1:T(8,128)}, f32[32,180,128]{2,0,1:T(8,128)}) fusion(f32[2,180,32,128]{3,2,1,0:T(8,128)} %shard_map.104), kind=kLoop, calls=%fused_computation | loop fusion | bytes 11796480 | tf_op jit(solution)/shard_map/transpose | solution.py:582
